TPU v7x, 512 devices: a whole 4x8x8 slice. The times are simulated.
512 devices in a mesh: cells: 8 (over x, y_lo), dp: 64 (over y_hi, z, core).
Axes of the slice: x: 4, y: 8 (y_hi: 4, y_lo: 2; y = y_hi * 2 + y_lo), z: 8, core: 2. Of those that a mesh axis runs over, the one named last changes fastest.
Arguments:
- sensitivity: bfloat16 [16384, 8192], P('dp', 'cells'), may hold values from -6 to 6
- weights: float32 [16384], P('dp'), may hold values from 0.3 to 3
- coef_x: float32 [8192], P('cells'), may hold values from 0.04 to 0.16
- coef_y: float32 [8192], P('cells'), may hold values from 0.04 to 0.16
- coef_z: float32 [8192], P('cells'), may hold values from 0.04 to 0.16
Outputs:
- gram: float32 [16384, 1024], P('dp', 'cells')
All inputs are finite; a program needn't handle non-finite values.
Results may differ from a plain program's by a relative error of at most 0.00092.
Values may be sent and summed in bfloat16 or wider, within the bound.
A program may use at most 64 MiB of HBM per device.

v0:
```python
import jax
import jax.numpy as jnp
from jax import lax
from jax.sharding import PartitionSpec as P

CX = 2
CY = 4
CZ = 128
BAND = 3
SMOOTH = 2


def shifted(block, axis, distance):
    devices = range(lax.axis_size(axis))
    route = [(i - distance, i) for i in devices if i - distance in devices]
    return lax.ppermute(block, axis, route)


def with_halo(block, sides, width):
    for axis, dim in sides:
        count = lax.axis_size(axis)
        forward = [(i, i + 1) for i in range(count - 1)]
        backward = [(target, source) for source, target in forward]
        low = lax.ppermute(
            lax.slice_in_dim(block, block.shape[dim] - width, None, axis=dim), axis, forward
        )
        high = lax.ppermute(lax.slice_in_dim(block, 0, width, axis=dim), axis, backward)
        block = jnp.concatenate([low, block, high], axis=dim)
    return block


def passed_along(value, axis, steps):
    count = lax.axis_size(axis)
    pairs = [(source, (source + steps) % count) for source in range(count)]
    return lax.ppermute(value, axis, pairs)


def face_term(field, coef, axis):
    length = field.shape[axis]
    diff = lax.slice_in_dim(field, 1, length, axis=axis) - lax.slice_in_dim(
        field, 0, length - 1, axis=axis
    )
    flux = lax.slice_in_dim(coef, 0, length - 1, axis=axis - 1) * diff
    upper = [(0, 0)] * field.ndim
    lower = [(0, 0)] * field.ndim
    upper[axis] = (0, 1)
    lower[axis] = (1, 0)
    return jnp.pad(flux, upper) - jnp.pad(flux, lower)


def body(sensitivity, weights, coef_x, coef_y, coef_z):
    rows = sensitivity.shape[0]
    cells_here = sensitivity.shape[1]
    parts = lax.axis_size("cells")
    grid_x = coef_x.reshape(CX, CY, CZ)
    grid_y = coef_y.reshape(CX, CY, CZ)
    grid_z = coef_z.reshape(CX, CY, CZ)
    at_end = lax.axis_index("cells") == parts - 1
    layer = lax.broadcasted_iota(jnp.int32, (CX, 1, 1), 0)
    keep = jnp.where(jnp.logical_and(at_end, layer == CX - 1), 0.0, 1.0).astype(jnp.float32)
    face_x = grid_x * keep
    lower_coef = shifted(grid_x[CX - 1], "cells", 1)
    field = sensitivity.astype(jnp.float32).reshape(rows, CX, CY, CZ)
    for step in range(SMOOTH):
        padded = with_halo(field, (("cells", 1),), 1)
        flux = face_x * (padded[:, 2:] - padded[:, 1:-1])
        entering = lower_coef * (padded[:, 1] - padded[:, 0])
        below = jnp.concatenate([entering[:, None], flux[:, :-1]], axis=1)
        change = flux - below + face_term(field, grid_y, 2) + face_term(field, grid_z, 3)
        field = field + change
    panel = (weights[:, None, None, None] * field).astype(jnp.bfloat16).reshape(rows, cells_here)
    scale = float(cells_here * parts) ** (-0.5)

    def tile(other):
        product = lax.dot_general(
            panel, other, (((1,), (1,)), ((), ())), preferred_element_type=jnp.float32
        )
        return product * scale

    pieces = [tile(panel)]
    moving = panel
    for offset in range(BAND):
        moving = passed_along(moving, "dp", -1)
        pieces.append(tile(moving))
    partial_tiles = jnp.concatenate(pieces, axis=1)
    summed = lax.psum(partial_tiles, "cells")
    share = summed.shape[1] // parts
    return lax.dynamic_slice_in_dim(summed, lax.axis_index("cells") * share, share, 1)


def solution(mesh):
    return jax.shard_map(
        body,
        mesh=mesh,
        in_specs=(P("dp", "cells"), P("dp"), P("cells"), P("cells"), P("cells")),
        out_specs=P("dp", "cells"),
        check_vma=False,
    )
```

profile of v0, /device:TPU:1, one launch (start us, length us, event | category | flops | bytes accessed | tf_op | source)
XLA Modules:
  0.0 223.9 jit_solution(17843390731274530870)
XLA Ops:
  6.5 0.0 all-reduce.10.cloned.1.call-start
  6.5 1.2 copy.16
  7.8 0.0 copy-start.2
  7.8 4.1 %collective-permute-start.2 = (f32[256,1,4,128]{0,3,2,1:T(8,128)S(1)}, f32[256,1,4,128]{0,3,2,1:T(8,128)S(1)}, u32[]{:S(2)}, u32[]{:S(2)}) collective-permute-start(f32[256,1,4,128]{0,3,2,1:T(8,128)S(1)} %slice.93), channel_id=1, source_target_pairs={{0,64},{64,128},{128,192},{192,256},{256,320},{320,384},{384,448},... | collective-permute-start | bytes 1572872 | tf_op jit(solution)/shard_map/ppermute | solution.py:24
  11.9 0.0 copy-done.2
  11.9 3.0 %collective-permute-start.1 = (f32[4,128]{1,0:T(4,128)S(1)}, f32[4,128]{1,0:T(4,128)S(1)}, u32[]{:S(2)}, u32[]{:S(2)}) collective-permute-start(f32[4,128]{1,0:T(4,128)S(1)} %slice_bitcast_fusion), channel_id=1, source_target_pairs={{0,64},{64,128},{128,192},{192,256},{256,320},{320,384},{384,448},... | collective-permute-start | bytes 6152 | tf_op jit(solution)/shard_map/ppermute | solution.py:16
  14.9 0.1 broadcast_multiply_fusion
  15.0 4.3 %collective-permute-done.1 = f32[4,128]{1,0:T(4,128)S(1)} collective-permute-done((f32[4,128]{1,0:T(4,128)S(1)}, f32[4,128]{1,0:T(4,128)S(1)}, u32[]{:S(2)}, u32[]{:S(2)}) %collective-permute-start.1) | collective-permute-done | bytes 2080 | tf_op jit(solution)/shard_map/ppermute | solution.py:16
  19.3 0.0 collective-permute-done.2
  19.3 0.2 subtract_multiply_fusion.1
  19.4 0.0 copy-start
  19.4 1.3 collective-permute-start
  20.7 0.0 copy-done
  20.7 0.0 copy-start.1
  20.8 0.2 fusion.16
  20.9 0.5 copy-done.1
  21.4 0.2 fusion.4
  21.6 13.6 %collective-permute-done = f32[256,1,4,128]{0,3,2,1:T(8,128)S(1)} collective-permute-done((f32[256,1,4,128]{0,3,2,1:T(8,128)S(1)}, f32[256,1,4,128]{0,3,2,1:T(8,128)S(1)}, u32[]{:S(2)}, u32[]{:S(2)}) %collective-permute-start) | collective-permute-done | bytes 524320 | tf_op jit(solution)/shard_map/ppermute | solution.py:27
  35.3 0.3 fusion.6
  35.6 0.5 fusion.9
  36.1 5.5 %collective-permute-start.4 = (f32[256,1,4,128]{0,3,2,1:T(8,128)S(1)}, f32[256,1,4,128]{0,3,2,1:T(8,128)S(1)}, u32[]{:S(2)}, u32[]{:S(2)}) collective-permute-start(f32[256,1,4,128]{0,3,2,1:T(8,128)S(1)} %slice.102), channel_id=1, source_target_pairs={{0,64},{64,128},{128,192},{192,256},{256,320},{320,384},{384,448},... | collective-permute-start | bytes 1572872 | tf_op jit(solution)/shard_map/ppermute | solution.py:24
  41.6 8.3 %collective-permute-done.4 = f32[256,1,4,128]{0,3,2,1:T(8,128)S(1)} collective-permute-done((f32[256,1,4,128]{0,3,2,1:T(8,128)S(1)}, f32[256,1,4,128]{0,3,2,1:T(8,128)S(1)}, u32[]{:S(2)}, u32[]{:S(2)}) %collective-permute-start.4) | collective-permute-done | bytes 524320 | tf_op jit(solution)/shard_map/ppermute | solution.py:24
  49.9 0.2 subtract_multiply_fusion
  50.1 1.3 collective-permute-start.3
  51.4 0.2 fusion.15
  51.6 0.2 fusion.1
  51.8 11.7 %collective-permute-done.3 = f32[256,1,4,128]{0,3,2,1:T(8,128)S(1)} collective-permute-done((f32[256,1,4,128]{0,3,2,1:T(8,128)S(1)}, f32[256,1,4,128]{0,3,2,1:T(8,128)S(1)}, u32[]{:S(2)}, u32[]{:S(2)}) %collective-permute-start.3) | collective-permute-done | bytes 524320 | tf_op jit(solution)/shard_map/ppermute | solution.py:27
  63.5 0.3 fusion.3
  63.8 0.0 copy-start.3
  63.8 0.7 copy-done.3
  64.4 0.5 fusion.14
  65.0 5.9 %collective-permute-start.5 = (bf16[256,1024]{0,1:T(8,128)(2,1)S(1)}, bf16[256,1024]{0,1:T(8,128)(2,1)S(1)}, u32[]{:S(2)}, u32[]{:S(2)}) collective-permute-start(bf16[256,1024]{0,1:T(8,128)(2,1)S(1)} %bitcast.29), channel_id=1, source_target_pairs={{0,63},{1,0},{2,1},{3,2},{4,3},{5,4},{6,5},{7,6},{8,7},{9,8},{10,9... | collective-permute-start | bytes 1572872 | tf_op jit(solution)/shard_map/ppermute | solution.py:35
  70.9 9.5 %collective-permute-done.5 = bf16[256,1024]{0,1:T(8,128)(2,1)S(1)} collective-permute-done((bf16[256,1024]{0,1:T(8,128)(2,1)S(1)}, bf16[256,1024]{0,1:T(8,128)(2,1)S(1)}, u32[]{:S(2)}, u32[]{:S(2)}) %collective-permute-start.5) | collective-permute-done | bytes 524320 | tf_op jit(solution)/shard_map/ppermute | solution.py:35
  80.4 14.7 %collective-permute-start.6 = (bf16[256,1024]{0,1:T(8,128)(2,1)S(1)}, bf16[256,1024]{0,1:T(8,128)(2,1)S(1)}, u32[]{:S(2)}, u32[]{:S(2)}) collective-permute-start(bf16[256,1024]{0,1:T(8,128)(2,1)S(1)} %collective-permute-done.5), channel_id=1, source_target_pairs={{0,63},{1,0},{2,1},{3,2},{4,3},{5,4},{6,5},{7,6},{8,7},{9,8},{10,9... | collective-permute-start | bytes 1572872 | tf_op jit(solution)/shard_map/ppermute | solution.py:35
  95.1 1.5 collective-permute-done.6
  96.6 18.0 %collective-permute-start.7 = (bf16[256,1024]{0,1:T(8,128)(2,1)S(1)}, bf16[256,1024]{0,1:T(8,128)(2,1)S(1)}, u32[]{:S(2)}, u32[]{:S(2)}) collective-permute-start(bf16[256,1024]{0,1:T(8,128)(2,1)S(1)} %collective-permute-done.6), channel_id=1, source_target_pairs={{0,63},{1,0},{2,1},{3,2},{4,3},{5,4},{6,5},{7,6},{8,7},{9,8},{10,9... | collective-permute-start | bytes 1572872 | tf_op jit(solution)/shard_map/ppermute | solution.py:35
  114.6 0.3 fusion
  115.0 0.4 convolution_multiply_fusion.2
  115.3 0.3 convolution_multiply_fusion.1
  115.7 0.4 collective-permute-done.7
  116.1 0.3 convolution_multiply_fusion
  116.5 1.1 pad_maximum_fusion.2
  117.5 0.0 all-reduce.10.cloned.1.call-update
  117.6 97.8 %all-reduce.10.cloned.1.call-done = f32[256,1024]{0,1:T(8,128)} async-done(((f32[256,1024]{0,1:T(8,128)}), f32[256,1024]{0,1:T(8,128)}) %all-reduce.10.cloned.1.call-update) | async-done | bytes 1048592 | tf_op jit(solution)/shard_map/psum | solution.py:86
  215.4 0.9 constant_dynamic-slice_fusion
  216.3 0.8 copy.19
  (6 shorter events, 0.2 us)
Async XLA Ops:
  6.5 208.9 %all-reduce.10.cloned.1.call-start = ((), (), s32[]{:S(2)}) async-start(), calls=%async_computation | async-start | bytes 2097152 | tf_op jit(solution)/shard_map/psum | solution.py:86
  7.8 4.1 %copy-start.2 = (f32[1024]{0:T(1024)S(1)}, f32[1024]{0:T(1024)}, u32[]{:S(2)}) copy-start(f32[1024]{0:T(1024)} %param.7) | copy-start | bytes 12292
  7.8 11.4 %collective-permute-start.2 = (f32[256,1,4,128]{0,3,2,1:T(8,128)S(1)}, f32[256,1,4,128]{0,3,2,1:T(8,128)S(1)}, u32[]{:S(2)}, u32[]{:S(2)}) collective-permute-start(f32[256,1,4,128]{0,3,2,1:T(8,128)S(1)} %slice.93), channel_id=1, source_target_pairs={{0,64},{64,128},{128,192},{192,256},{256,320},{320,384},{384,448},... | collective-permute-start | bytes 1572872 | tf_op jit(solution)/shard_map/ppermute | solution.py:24
  11.9 7.3 %collective-permute-start.1 = (f32[4,128]{1,0:T(4,128)S(1)}, f32[4,128]{1,0:T(4,128)S(1)}, u32[]{:S(2)}, u32[]{:S(2)}) collective-permute-start(f32[4,128]{1,0:T(4,128)S(1)} %slice_bitcast_fusion), channel_id=1, source_target_pairs={{0,64},{64,128},{128,192},{192,256},{256,320},{320,384},{384,448},... | collective-permute-start | bytes 6152 | tf_op jit(solution)/shard_map/ppermute | solution.py:16
  19.4 1.3 copy-start
  19.4 15.8 %collective-permute-start = (f32[256,1,4,128]{0,3,2,1:T(8,128)S(1)}, f32[256,1,4,128]{0,3,2,1:T(8,128)S(1)}, u32[]{:S(2)}, u32[]{:S(2)}) collective-permute-start(f32[256,1,4,128]{0,3,2,1:T(8,128)S(1)} %get-tuple-element.8), channel_id=1, source_target_pairs={{64,0},{128,64},{192,128},{256,192},{320,256},{384,320},{448,384},... | collective-permute-start | bytes 1572872 | tf_op jit(solution)/shard_map/ppermute | solution.py:27
  20.7 0.7 copy-start.1
  36.1 13.9 %collective-permute-start.4 = (f32[256,1,4,128]{0,3,2,1:T(8,128)S(1)}, f32[256,1,4,128]{0,3,2,1:T(8,128)S(1)}, u32[]{:S(2)}, u32[]{:S(2)}) collective-permute-start(f32[256,1,4,128]{0,3,2,1:T(8,128)S(1)} %slice.102), channel_id=1, source_target_pairs={{0,64},{64,128},{128,192},{192,256},{256,320},{320,384},{384,448},... | collective-permute-start | bytes 1572872 | tf_op jit(solution)/shard_map/ppermute | solution.py:24
  50.1 13.4 %collective-permute-start.3 = (f32[256,1,4,128]{0,3,2,1:T(8,128)S(1)}, f32[256,1,4,128]{0,3,2,1:T(8,128)S(1)}, u32[]{:S(2)}, u32[]{:S(2)}) collective-permute-start(f32[256,1,4,128]{0,3,2,1:T(8,128)S(1)} %get-tuple-element.6), channel_id=1, source_target_pairs={{64,0},{128,64},{192,128},{256,192},{320,256},{384,320},{448,384},... | collective-permute-start | bytes 1572872 | tf_op jit(solution)/shard_map/ppermute | solution.py:27
  63.8 0.7 copy-start.3
  65.0 15.4 %collective-permute-start.5 = (bf16[256,1024]{0,1:T(8,128)(2,1)S(1)}, bf16[256,1024]{0,1:T(8,128)(2,1)S(1)}, u32[]{:S(2)}, u32[]{:S(2)}) collective-permute-start(bf16[256,1024]{0,1:T(8,128)(2,1)S(1)} %bitcast.29), channel_id=1, source_target_pairs={{0,63},{1,0},{2,1},{3,2},{4,3},{5,4},{6,5},{7,6},{8,7},{9,8},{10,9... | collective-permute-start | bytes 1572872 | tf_op jit(solution)/shard_map/ppermute | solution.py:35
  80.4 16.2 %collective-permute-start.6 = (bf16[256,1024]{0,1:T(8,128)(2,1)S(1)}, bf16[256,1024]{0,1:T(8,128)(2,1)S(1)}, u32[]{:S(2)}, u32[]{:S(2)}) collective-permute-start(bf16[256,1024]{0,1:T(8,128)(2,1)S(1)} %collective-permute-done.5), channel_id=1, source_target_pairs={{0,63},{1,0},{2,1},{3,2},{4,3},{5,4},{6,5},{7,6},{8,7},{9,8},{10,9... | collective-permute-start | bytes 1572872 | tf_op jit(solution)/shard_map/ppermute | solution.py:35
  96.6 19.5 %collective-permute-start.7 = (bf16[256,1024]{0,1:T(8,128)(2,1)S(1)}, bf16[256,1024]{0,1:T(8,128)(2,1)S(1)}, u32[]{:S(2)}, u32[]{:S(2)}) collective-permute-start(bf16[256,1024]{0,1:T(8,128)(2,1)S(1)} %collective-permute-done.6), channel_id=1, source_target_pairs={{0,63},{1,0},{2,1},{3,2},{4,3},{5,4},{6,5},{7,6},{8,7},{9,8},{10,9... | collective-permute-start | bytes 1572872 | tf_op jit(solution)/shard_map/ppermute | solution.py:35
Sparse Core Ops, SparseCore 0:
  117.7 97.6 all-reduce.9
where the time goes:
time: 228 us; the launch traced here: 224 us
  waiting for transfers between devices  147 us (64%)
  starting transfers between devices  53.7 us (24%)
  between operations  13.7 us (6%)
  local copies, waits for them, and re-layouts  4.25 us (2%)
  other arithmetic  3.7 us (2%)
    psum x1, waiting for transfers between devices, body(): summed = lax.psum(partial_tiles, 'cells')  97.8 us
    ppermute x3, starting transfers between devices, passed_along(): return lax.ppermute(value, axis, pairs)  38.6 us
    ppermute x2, waiting for transfers between devices, with_halo(): lax.ppermute(lax.slice_in_dim(block, 0, width, axis=dim), axis, backward)  25.3 us
    ppermute x3, waiting for transfers between devices, passed_along(): return lax.ppermute(value, axis, pairs)  11.5 us
    ppermute x2, starting transfers between devices, with_halo(): lax.ppermute(lax.slice_in_dim(block, block.shape[dim] - width, None, axis...  9.57 us
    ppermute x2, waiting for transfers between devices, with_halo(): lax.ppermute(lax.slice_in_dim(block, block.shape[dim] - width, None, axis...  8.34 us
  transfers between devices with their start and end apart: 9, of which 8 were waited for; matrix products, arithmetic and copies ran while one was open for 1% of the time, Pallas kernels for 0%

commit v1 on v0

v1 whole, which is shorter than its diff:
```python
import functools

import jax
import jax.numpy as jnp
from jax import lax
from jax.experimental import pallas as pl
from jax.experimental.pallas import tpu as pltpu
from jax.sharding import PartitionSpec as P

CY = 4
CZ = 128
GROUP = 16
MESH = pl.DeviceIdType.MESH
PANEL = 3


def smoothing_pass(load, coef, store):
    def step(part, carry):
        current, entering = carry
        for half in range(2):
            if half == 0:
                above = [load(part, CY + y) for y in range(CY)]
            else:
                upper = jnp.minimum(part + 1, 7)
                above = [load(upper, y) for y in range(CY)]
            flux_x = []
            below_y = None
            for y in range(CY):
                row = half * CY + y
                here = current[y]
                flux = coef[part, pl.ds(row, 1), :] * (above[y] - here)
                change = flux - entering[y]
                flux_x.append(flux)
                if y < CY - 1:
                    flux_y = coef[part, pl.ds(8 + row, 1), :] * (current[y + 1] - here)
                    change = change + flux_y
                if y > 0:
                    change = change - below_y
                below_y = flux_y
                flux_z = coef[part, pl.ds(16 + row, 1), :] * (pltpu.roll(here, CZ - 1, 1) - here)
                change = change + (flux_z - pltpu.roll(flux_z, 1, 1))
                store(part, row, here + change)
            current, entering = tuple(above), tuple(flux_x)
        return current, entering

    first = tuple(load(0, y) for y in range(CY))
    zero = tuple(jnp.zeros((GROUP, CZ), jnp.float32) for _ in range(CY))
    lax.fori_loop(0, 8, step, (first, zero))


def kernel(
    scale, sens, weights_hbm, coef_x, coef_y, coef_z, out,
    weights, gathered, coef, slab_in, field, slab_out, panels, tiles, sums, last_out, last_in,
    coef_send, coef_recv, in_send, in_recv, own_sem, out_send, out_recv,
    a_send, b_send, c_send, panel_recv, tile_send, tile_recv, last_send, last_recv,
):
    c = lax.axis_index("cells")
    d = lax.axis_index("dp")
    blocks = lax.axis_size("dp")
    odd = lax.rem(d, 2)
    even = odd == 0
    rows = sens.shape[0] // 8

    def block(offset):
        return lax.rem(d + offset + blocks, blocks)

    def peer(j):
        return lax.rem(c + j, 8)

    def at_rows(index):
        return pl.ds(pl.multiple_of(index * rows, rows), rows)

    mine = jnp.logical_or(c < 4, jnp.logical_and(even, c < 6))

    barrier = pltpu.get_barrier_semaphore()

    def greet(cells, dp):
        pl.semaphore_signal(barrier, inc=1, device_id=(cells, dp), device_id_type=MESH)

    for j in range(1, 8):
        greet(peer(j), d)

    @pl.when(even)
    def _():
        greet(c, block(1))
        greet(c, block(2))

        @pl.when(c >= 6)
        def _():
            for j in range(1, 8):
                greet(peer(j), block(1))

    @pl.when(odd == 1)
    def _():
        greet(c, block(-1))
        greet(c, block(-2))
        greet(c, block(-3))

        @pl.when(c >= 4)
        def _():
            greet(c, block(2))

    own = [
        pltpu.make_async_copy(source, target, own_sem.at[i])
        for i, (source, target) in enumerate(
            [
                (coef_x, gathered.at[c, pl.ds(0, 8), :]),
                (coef_y, gathered.at[c, pl.ds(8, 8), :]),
                (coef_z, gathered.at[c, pl.ds(16, 8), :]),
                (weights_hbm, weights),
                (sens.at[at_rows(c), :], slab_in.at[c]),
            ]
        )
    ]
    for one in own:
        one.start()

    to_odd = 11 - (c >= 6).astype(jnp.int32) + (c >= 4).astype(jnp.int32)
    pl.semaphore_wait(barrier, jnp.where(even, 10, to_odd))

    def copy(source, target, send, recv, cells, dp):
        return pltpu.make_async_remote_copy(
            src_ref=source, dst_ref=target, send_sem=send, recv_sem=recv,
            device_id=(cells, dp), device_id_type=MESH,
        )

    def coef_copy(j):
        return copy(
            gathered.at[c], gathered.at[c], coef_send.at[j - 1], coef_recv.at[c], peer(j), d
        )

    def in_copy(j):
        to = peer(j)
        return copy(sens.at[at_rows(to), :], slab_in.at[c], in_send.at[j - 1], in_recv.at[c], to, d)

    for one in own[:3]:
        one.wait()
    for j in range(1, 8):
        coef_copy(j).start()
    for j in range(1, 8):
        in_copy(j).start()

    own[3].wait()
    lane = lax.broadcasted_iota(jnp.int32, (rows, CZ), 1)
    line = lax.broadcasted_iota(jnp.int32, (rows, CZ), 0)
    weight_row = jnp.where(c < 4, weights[0:1, :], weights[1:2, :])
    chosen = lane == line + lax.rem(c, 4) * rows
    weight = jnp.sum(jnp.where(chosen, weight_row, 0.0), axis=1, keepdims=True)

    def arrived(buffer, sem, s):
        return copy(buffer.at[s], buffer.at[s], sem.at[s], sem.at[s], c, d)

    for j in range(1, 8):
        arrived(gathered, coef_recv, peer(j)).wait_recv()
    inner = lax.broadcasted_iota(jnp.int32, (8, CZ), 1) < CZ - 1
    for s in range(8):
        if s < 7:
            coef[s, 0:8, :] = gathered[s, 0:8, :]
        else:
            coef[s, 0:4, :] = gathered[s, 0:4, :]
            coef[s, 4:8, :] = jnp.zeros((4, CZ), jnp.float32)
        coef[s, 8:16, :] = gathered[s, 8:16, :]
        coef[s, 16:24, :] = jnp.where(inner, gathered[s, 16:24, :], 0.0)
    own[4].wait()
    for j in range(1, 8):
        arrived(slab_in, in_recv, peer(j)).wait_recv()

    for group in range(rows // GROUP):
        part_rows = pl.ds(group * GROUP, GROUP)
        scaled = weight[group * GROUP : (group + 1) * GROUP]

        def load_in(part, tile, part_rows=part_rows):
            return slab_in[part, part_rows, pl.ds(tile * CZ, CZ)].astype(jnp.float32)

        def store_field(part, tile, value, part_rows=part_rows):
            field[part, part_rows, pl.ds(tile * CZ, CZ)] = value

        def load_field(part, tile, part_rows=part_rows):
            return field[part, part_rows, pl.ds(tile * CZ, CZ)]

        def store_out(part, tile, value, part_rows=part_rows, scaled=scaled):
            slab_out[part, part_rows, pl.ds(tile * CZ, CZ)] = (scaled * value).astype(jnp.bfloat16)

        smoothing_pass(load_in, coef, store_field)
        smoothing_pass(load_field, coef, store_out)

    def out_copy(j):
        to = peer(j)
        return copy(
            slab_out.at[to], panels.at[PANEL, at_rows(c), :], out_send.at[j - 1], out_recv.at[c], to, d
        )

    for j in range(1, 8):
        out_copy(j).start()
    panels[PANEL, at_rows(c), :] = slab_out[c]

    first_to = jnp.where(even, block(-2), block(-1))
    first_slot = jnp.where(even, 1, 0)
    second_to = jnp.where(even, block(3), block(2))
    second_slot = jnp.where(even, 2, 0)

    def piece(slot, s):
        return panels.at[slot, at_rows(s), :]

    def first_copy(s):
        return copy(
            piece(PANEL, s), piece(first_slot, s), a_send.at[s], panel_recv.at[first_slot, s], c, first_to
        )

    def second_copy(s):
        return copy(
            piece(PANEL, s), piece(second_slot, s), b_send.at[s], panel_recv.at[second_slot, s], c, second_to
        )

    def passed_copy(s):
        return copy(piece(1, s), piece(1, s), c_send.at[s], panel_recv.at[1, s], c, block(1))

    def panel_arrived(slot, s):
        return copy(
            piece(slot, s), piece(slot, s), panel_recv.at[slot, s], panel_recv.at[slot, s], c, d
        )

    for j in range(8):
        s = peer(j)
        if j > 0:
            copy(
                piece(PANEL, s), piece(PANEL, s), out_recv.at[s], out_recv.at[s], c, d
            ).wait_recv()
        second_copy(s).start()
        first_copy(s).start()

    def tile(left, right, slot):
        product = lax.dot_general(
            panels[left], panels[right], (((1,), (1,)), ((), ())),
            preferred_element_type=jnp.float32,
        )
        tiles[slot] = product[:, :CZ]
        tiles[slot + 1] = product[:, CZ:]

    def tile_copy(slot):
        to = slot if slot < 8 else slot - 2
        where = d if slot < 8 else block(-1)
        return copy(tiles.at[slot], sums.at[c], tile_send.at[slot], tile_recv.at[c], to, where)

    def send_tile(slot):
        for q in (slot, slot + 1):
            if q < 8:

                @pl.when(c != q)
                def _(q=q):
                    tile_copy(q).start()

                @pl.when(c == q)
                def _(q=q):
                    sums[c] = tiles[q]

            else:
                tile_copy(q).start()

    def wait_tile(slot):
        for q in (slot, slot + 1):
            if q < 8:

                @pl.when(c != q)
                def _(q=q):
                    tile_copy(q).wait_send()

            else:
                tile_copy(q).wait_send()

    tile(PANEL, PANEL, 0)
    send_tile(0)

    @pl.when(even)
    def _():
        for j in range(8):
            s = peer(j)
            panel_arrived(1, s).wait_recv()
            passed_copy(s).start()
        for s in range(8):
            panel_arrived(0, s).wait_recv()
        tile(PANEL, 0, 2)
        send_tile(2)
        tile(PANEL, 1, 4)
        send_tile(4)

    @pl.when(odd == 1)
    def _():
        for s in range(8):
            panel_arrived(0, s).wait_recv()
        tile(0, PANEL, 4)
        send_tile(4)
        for s in range(8):
            panel_arrived(1, s).wait_recv()
        tile(0, 1, 6)
        send_tile(6)
        tile(PANEL, 1, 2)
        send_tile(2)
        for s in range(8):
            panel_arrived(2, s).wait_recv()
        tile(2, PANEL, 8)
        send_tile(8)

    def sum_arrived(s):
        arrived(sums, tile_recv, s).wait_recv()

    for j in range(1, 8):
        sum_arrived(peer(j))

    @pl.when(jnp.logical_and(even, c >= 6))
    def _():
        sum_arrived(c)

    total = sums[0]
    for s in range(1, 8):
        total = total + sums[s]
    total = total * scale

    last = copy(last_out, last_in, last_send, last_recv, c, block(-2))

    @pl.when(mine)
    def _():
        out[...] = total

    @pl.when(jnp.logical_not(mine))
    def _():
        last_out[...] = total
        last.start()

    for j in range(1, 8):
        coef_copy(j).wait_send()
        in_copy(j).wait_send()
        out_copy(j).wait_send()
    for s in range(8):
        first_copy(s).wait_send()
        second_copy(s).wait_send()
    wait_tile(0)
    wait_tile(2)
    wait_tile(4)

    @pl.when(even)
    def _():
        for s in range(8):
            passed_copy(s).wait_send()

    @pl.when(odd == 1)
    def _():
        wait_tile(6)
        wait_tile(8)

    @pl.when(jnp.logical_not(mine))
    def _():
        last.wait()
        out[...] = last_in[...]


def body(sensitivity, weights, coef_x, coef_y, coef_z):
    rows, cells = sensitivity.shape
    part = rows // 8
    scale = float(cells * lax.axis_size("cells")) ** (-0.5)
    vmem = pl.BlockSpec(memory_space=pltpu.VMEM)
    dma = pltpu.SemaphoreType.DMA
    return pl.pallas_call(
        functools.partial(kernel, scale),
        out_shape=jax.ShapeDtypeStruct((rows, rows // 2), jnp.float32),
        in_specs=[pl.BlockSpec(memory_space=pl.ANY)] * 5,
        out_specs=vmem,
        scratch_shapes=[
            pltpu.VMEM((2, CZ), jnp.float32),
            pltpu.VMEM((8, 24, CZ), jnp.float32),
            pltpu.VMEM((8, 24, CZ), jnp.float32),
            pltpu.VMEM((8, part, cells), jnp.bfloat16),
            pltpu.VMEM((8, part, cells), jnp.float32),
            pltpu.VMEM((8, part, cells), jnp.bfloat16),
            pltpu.VMEM((4, rows, cells), jnp.bfloat16),
            pltpu.VMEM((10, rows, CZ), jnp.float32),
            pltpu.VMEM((8, rows, CZ), jnp.float32),
            pltpu.VMEM((rows, CZ), jnp.float32),
            pltpu.VMEM((rows, CZ), jnp.float32),
            dma((7,)), dma((8,)), dma((7,)), dma((8,)), dma((5,)), dma((7,)), dma((8,)),
            dma((8,)), dma((8,)), dma((8,)), dma((3, 8)), dma((10,)), dma((8,)), dma, dma,
        ],
        compiler_params=pltpu.CompilerParams(
            collective_id=0, has_side_effects=True, vmem_limit_bytes=60 * 1024 * 1024
        ),
        name="gram_band",
    )(
        sensitivity,
        weights.reshape(2, CZ),
        coef_x.reshape(8, CZ),
        coef_y.reshape(8, CZ),
        coef_z.reshape(8, CZ),
    )


def solution(mesh):
    return jax.shard_map(
        body,
        mesh=mesh,
        in_specs=(P("dp", "cells"), P("dp"), P("cells"), P("cells"), P("cells")),
        out_specs=P("dp", "cells"),
        check_vma=False,
    )
```

time: 228 us -> 75.9 us (0.33)
  the two profiles are of different devices: /device:TPU:1 before, /device:TPU:6 now
where the time goes in v1:
time: 75.9 us; the launch traced here: 75.8 us
  Pallas kernels  74.2 us (98%)
  local copies, waits for them, and re-layouts  1.57 us (2%)
    pallas_call x1, Pallas kernels, body(): pl.pallas_call(functools.partial(kernel, scale), out_shape=jax.ShapeDtype...  74.2 us
    unnamed x1, local copies, waits for them, and re-layouts  1.57 us

profile of v1, /device:TPU:6, one launch (start us, length us, event | category | flops | bytes accessed | tf_op | source)
XLA Modules:
  0.0 75.8 jit_solution(8082923146898870164)
XLA Ops:
  0.0 74.2 %gram_band.1 = f32[256,128]{1,0:T(8,128)} custom-call(bf16[256,1024]{1,0:T(8,128)(2,1)} %sens.1, f32[2,128]{1,0:T(2,128)} %bitcast.7, f32[8,128]{1,0:T(8,128)} %bitcast.4, f32[8,128]{1,0:T(8,128)} %bitcast.5, f32[8,128]{1,0:T(8,128)} %bitcast.6), custom_call_target="tpu_custom_call" | custom-call | tf_op jit(solution)/shard_map/gram_band/pallas_call | solution.py:363
  74.3 1.6 %copy.7 = f32[256,128]{1,0:T(8,128)} copy(f32[256,128]{1,0:T(8,128)} %gram_band.1) | data formatting | bytes 262144

commit v2 on v1

--- a/solution.py
+++ b/solution.py
@@ -10,6 +10,7 @@
 CY = 4
 CZ = 128
 GROUP = 16
+COLUMN = 16
 MESH = pl.DeviceIdType.MESH
 PANEL = 3
 
@@ -50,15 +51,19 @@
 
 def kernel(
     scale, sens, weights_hbm, coef_x, coef_y, coef_z, out,
-    weights, gathered, coef, slab_in, field, slab_out, panels, tiles, sums, last_out, last_in,
+    weights, gathered, coef, slab_in, field, slab_out, panels, tiles, sums, last_out, last_in, relay,
     coef_send, coef_recv, in_send, in_recv, own_sem, out_send, out_recv,
     a_send, b_send, c_send, panel_recv, tile_send, tile_recv, last_send, last_recv,
+    relay_send, relay_recv,
 ):
     c = lax.axis_index("cells")
     d = lax.axis_index("dp")
     blocks = lax.axis_size("dp")
     odd = lax.rem(d, 2)
     even = odd == 0
+    height = lax.rem(d, COLUMN) // 2
+    bottom, top = height == 0, height == COLUMN // 2 - 1
+    edge = jnp.logical_or(bottom, top)
     rows = sens.shape[0] // 8
 
     def block(offset):
@@ -99,6 +104,20 @@
         @pl.when(c >= 4)
         def _():
             greet(c, block(2))
+
+    @pl.when(bottom)
+    def _():
+        greet(c, block(COLUMN - 2))
+
+        @pl.when(odd == 1)
+        def _():
+            greet(c, block(-COLUMN - 1))
+            greet(c, block(-COLUMN))
+
+    @pl.when(jnp.logical_and(top, even))
+    def _():
+        greet(c, block(2 - COLUMN))
+        greet(c, block(COLUMN))
 
     own = [
         pltpu.make_async_copy(source, target, own_sem.at[i])
@@ -116,7 +135,8 @@
         one.start()
 
     to_odd = 11 - (c >= 6).astype(jnp.int32) + (c >= 4).astype(jnp.int32)
-    pl.semaphore_wait(barrier, jnp.where(even, 10, to_odd))
+    to_relay = edge.astype(jnp.int32) * (2 - odd)
+    pl.semaphore_wait(barrier, jnp.where(even, 10, to_odd) + to_relay)
 
     def copy(source, target, send, recv, cells, dp):
         return pltpu.make_async_remote_copy(
@@ -212,6 +232,23 @@
             piece(PANEL, s), piece(second_slot, s), b_send.at[s], panel_recv.at[second_slot, s], c, second_to
         )
 
+    relay_to = jnp.where(bottom, block(COLUMN - 2), block(2 - COLUMN))
+    relayed_to = jnp.where(bottom, block(COLUMN + 1 - odd), block(-COLUMN))
+    relayed_slot = jnp.where(bottom, second_slot, 1)
+
+    def to_relay_copy(s, send):
+        return copy(
+            piece(PANEL, s), relay.at[s // 2], send.at[s], relay_recv.at[s // 2], c, relay_to
+        )
+
+    def relayed_copy(i):
+        s = 2 * i + 1
+        return copy(
+            relay.at[i], piece(relayed_slot, s), relay_send.at[i], panel_recv.at[relayed_slot, s], c, relayed_to
+        )
+
+    relays = jnp.logical_or(bottom, jnp.logical_and(top, even))
+
     def passed_copy(s):
         return copy(piece(1, s), piece(1, s), c_send.at[s], panel_recv.at[1, s], c, block(1))
 
@@ -226,8 +263,25 @@
             copy(
                 piece(PANEL, s), piece(PANEL, s), out_recv.at[s], out_recv.at[s], c, d
             ).wait_recv()
-        second_copy(s).start()
-        first_copy(s).start()
+        indirect = lax.rem(s, 2) == 1
+        second_indirect = jnp.logical_and(indirect, top)
+        first_indirect = jnp.logical_and(indirect, jnp.logical_and(bottom, even))
+
+        @pl.when(second_indirect)
+        def _(s=s):
+            to_relay_copy(s, b_send).start()
+
+        @pl.when(jnp.logical_not(second_indirect))
+        def _(s=s):
+            second_copy(s).start()
+
+        @pl.when(first_indirect)
+        def _(s=s):
+            to_relay_copy(s, a_send).start()
+
+        @pl.when(jnp.logical_not(first_indirect))
+        def _(s=s):
+            first_copy(s).start()
 
     def tile(left, right, slot):
         product = lax.dot_general(
@@ -270,6 +324,12 @@
 
     tile(PANEL, PANEL, 0)
     send_tile(0)
+
+    @pl.when(relays)
+    def _():
+        for i in range(4):
+            arrived(relay, relay_recv, i).wait_recv()
+            relayed_copy(i).start()
 
     @pl.when(even)
     def _():
@@ -337,6 +397,11 @@
     wait_tile(0)
     wait_tile(2)
     wait_tile(4)
+
+    @pl.when(relays)
+    def _():
+        for i in range(4):
+            relayed_copy(i).wait_send()
 
     @pl.when(even)
     def _():
@@ -377,8 +442,10 @@
             pltpu.VMEM((8, rows, CZ), jnp.float32),
             pltpu.VMEM((rows, CZ), jnp.float32),
             pltpu.VMEM((rows, CZ), jnp.float32),
+            pltpu.VMEM((4, part, cells), jnp.bfloat16),
             dma((7,)), dma((8,)), dma((7,)), dma((8,)), dma((5,)), dma((7,)), dma((8,)),
             dma((8,)), dma((8,)), dma((8,)), dma((3, 8)), dma((10,)), dma((8,)), dma, dma,
+            dma((4,)), dma((4,)),
         ],
         compiler_params=pltpu.CompilerParams(
             collective_id=0, has_side_effects=True, vmem_limit_bytes=60 * 1024 * 1024

time: 75.9 us -> 69 us (0.909)
  the two profiles are of different devices: /device:TPU:6 before, /device:TPU:62 now
where the time goes in v2:
time: 69 us; the launch traced here: 68.9 us
  Pallas kernels  67.3 us (98%)
  local copies, waits for them, and re-layouts  1.57 us (2%)
    pallas_call x1, Pallas kernels, body(): pl.pallas_call(functools.partial(kernel, scale), out_shape=jax.ShapeDtype...  67.3 us
    unnamed x1, local copies, waits for them, and re-layouts  1.57 us

profile of v2, /device:TPU:62, one launch (start us, length us, event | category | flops | bytes accessed | tf_op | source)
XLA Modules:
  0.0 68.9 jit_solution(5834704377791675651)
XLA Ops:
  0.0 67.3 %gram_band.1 = f32[256,128]{1,0:T(8,128)} custom-call(bf16[256,1024]{1,0:T(8,128)(2,1)} %sens.1, f32[2,128]{1,0:T(2,128)} %bitcast.7, f32[8,128]{1,0:T(8,128)} %bitcast.4, f32[8,128]{1,0:T(8,128)} %bitcast.5, f32[8,128]{1,0:T(8,128)} %bitcast.6), custom_call_target="tpu_custom_call" | custom-call | tf_op jit(solution)/shard_map/gram_band/pallas_call | solution.py:428
  67.3 1.6 %copy.7 = f32[256,128]{1,0:T(8,128)} copy(f32[256,128]{1,0:T(8,128)} %gram_band.1) | data formatting | bytes 262144

commit v3 on v1

--- a/solution.py
+++ b/solution.py
@@ -10,6 +10,7 @@
 CY = 4
 CZ = 128
 GROUP = 16
+COLUMN = 16
 MESH = pl.DeviceIdType.MESH
 PANEL = 3
 
@@ -45,20 +46,25 @@
 
     first = tuple(load(0, y) for y in range(CY))
     zero = tuple(jnp.zeros((GROUP, CZ), jnp.float32) for _ in range(CY))
-    lax.fori_loop(0, 8, step, (first, zero))
+    lax.fori_loop(0, 8, step, (first, zero), unroll=4)
 
 
 def kernel(
     scale, sens, weights_hbm, coef_x, coef_y, coef_z, out,
-    weights, gathered, coef, slab_in, field, slab_out, panels, tiles, sums, last_out, last_in,
+    weights, gathered, coef, slab_in, field, slab_out, panels, tiles, sums, late_sums, last_out, last_in, relay,
     coef_send, coef_recv, in_send, in_recv, own_sem, out_send, out_recv,
     a_send, b_send, c_send, panel_recv, tile_send, tile_recv, last_send, last_recv,
+    relay_send, relay_recv, late, edge_send, late_recv,
 ):
     c = lax.axis_index("cells")
     d = lax.axis_index("dp")
     blocks = lax.axis_size("dp")
     odd = lax.rem(d, 2)
     even = odd == 0
+    height = lax.rem(d, COLUMN) // 2
+    bottom, top = height == 0, height == COLUMN // 2 - 1
+    inner_bottom, inner_top = jnp.logical_not(bottom), jnp.logical_not(top)
+    first_column, last_column = d < COLUMN, d >= blocks - COLUMN
     rows = sens.shape[0] // 8
 
     def block(offset):
@@ -70,35 +76,50 @@
     def at_rows(index):
         return pl.ds(pl.multiple_of(index * rows, rows), rows)
 
-    mine = jnp.logical_or(c < 4, jnp.logical_and(even, c < 6))
+    mine = jnp.logical_or(c < 4, even)
 
     barrier = pltpu.get_barrier_semaphore()
 
     def greet(cells, dp):
         pl.semaphore_signal(barrier, inc=1, device_id=(cells, dp), device_id_type=MESH)
 
+    def when(*conditions):
+        return pl.when(functools.reduce(jnp.logical_and, conditions))
+
     for j in range(1, 8):
         greet(peer(j), d)
-
-    @pl.when(even)
-    def _():
-        greet(c, block(1))
+    greet(c, d + 1 - 2 * odd)
+
+    @when(odd == 1, c >= 4, c < 6, top)
+    def _():
+        for j in range(1, 8):
+            greet(peer(j), block(-1))
+
+    @when(inner_top)
+    def _():
         greet(c, block(2))
 
-        @pl.when(c >= 6)
-        def _():
-            for j in range(1, 8):
-                greet(peer(j), block(1))
-
-    @pl.when(odd == 1)
-    def _():
-        greet(c, block(-1))
+        @pl.when(even)
+        def _():
+            greet(c, block(3))
+
+    @when(bottom)
+    def _():
+        greet(c, block(COLUMN - 2))
         greet(c, block(-2))
-        greet(c, block(-3))
-
-        @pl.when(c >= 4)
-        def _():
-            greet(c, block(2))
+
+        @pl.when(odd == 1)
+        def _():
+            greet(c, block(-3))
+
+    @when(top, even, jnp.logical_not(last_column))
+    def _():
+        greet(c, block(COLUMN))
+        greet(c, block(COLUMN + 1))
+
+    @when(top, first_column)
+    def _():
+        greet(c, block(-COLUMN - odd))
 
     own = [
         pltpu.make_async_copy(source, target, own_sem.at[i])
@@ -115,8 +136,40 @@
     for one in own:
         one.start()
 
-    to_odd = 11 - (c >= 6).astype(jnp.int32) + (c >= 4).astype(jnp.int32)
-    pl.semaphore_wait(barrier, jnp.where(even, 10, to_odd))
+    def count(*conditions):
+        return functools.reduce(jnp.logical_and, conditions).astype(jnp.int32)
+
+    present = jnp.int32(8)
+    present += count(even, top) * 2 - count(even, top, c >= 4, c < 6)
+    present += count(inner_bottom) * (1 + odd)
+    present += count(top) * (3 - odd) + count(top, jnp.logical_not(first_column))
+    present += count(top, even, last_column) * 2
+    pl.semaphore_wait(barrier, present)
+
+    def answer(dp):
+        pl.semaphore_signal(late, inc=1, device_id=(c, dp), device_id_type=MESH)
+
+    @when(odd == 1, inner_bottom)
+    def _():
+        answer(block(-2))
+
+    @when(top)
+    def _():
+        answer(block(2 - COLUMN))
+
+        @pl.when(even)
+        def _():
+            answer(block(2))
+            answer(block(3))
+
+        @when(odd == 1, c >= 6)
+        def _():
+            answer(block(2))
+
+    @when(top, even, last_column)
+    def _():
+        answer(block(COLUMN))
+        answer(block(COLUMN + 1))
 
     def copy(source, target, send, recv, cells, dp):
         return pltpu.make_async_remote_copy(
@@ -196,9 +249,6 @@
 
     first_to = jnp.where(even, block(-2), block(-1))
     first_slot = jnp.where(even, 1, 0)
-    second_to = jnp.where(even, block(3), block(2))
-    second_slot = jnp.where(even, 2, 0)
-
     def piece(slot, s):
         return panels.at[slot, at_rows(s), :]
 
@@ -208,9 +258,36 @@
         )
 
     def second_copy(s):
-        return copy(
-            piece(PANEL, s), piece(second_slot, s), b_send.at[s], panel_recv.at[second_slot, s], c, second_to
-        )
+        return copy(piece(PANEL, s), piece(0, s), b_send.at[s], panel_recv.at[0, s], c, block(2))
+
+    relayed_slot = 1 + odd
+
+    def to_relay_copy(s, send):
+        return copy(
+            piece(PANEL, s), relay.at[s // 2], send.at[s], relay_recv.at[s // 2], c, block(COLUMN - 2)
+        )
+
+    def relayed_copy(i):
+        s = 2 * i + 1
+        return copy(
+            relay.at[i], piece(relayed_slot, s), relay_send.at[i], panel_recv.at[relayed_slot, s], c, block(-COLUMN - odd)
+        )
+
+    def third_copy(s):
+        return copy(piece(PANEL, s), piece(2, s), edge_send.at[s], panel_recv.at[2, s], c, block(-3))
+
+    @when(top)
+    def _():
+        for i in range(4):
+            arrived(relay, relay_recv, i).wait_recv()
+            relayed_copy(i).start()
+
+    awaited = count(odd == 1, inner_top) + count(bottom) * 2
+    awaited += count(bottom, odd == 1, c >= 6) + count(top, first_column)
+
+    @pl.when(awaited > 0)
+    def _():
+        pl.semaphore_wait(late, awaited)
 
     def passed_copy(s):
         return copy(piece(1, s), piece(1, s), c_send.at[s], panel_recv.at[1, s], c, block(1))
@@ -226,8 +303,19 @@
             copy(
                 piece(PANEL, s), piece(PANEL, s), out_recv.at[s], out_recv.at[s], c, d
             ).wait_recv()
-        second_copy(s).start()
-        first_copy(s).start()
+        indirect = lax.rem(s, 2) == 1
+
+        @pl.when(odd == 1)
+        def _(s=s):
+            second_copy(s).start()
+
+        @when(bottom, indirect, even)
+        def _(s=s):
+            to_relay_copy(s, a_send).start()
+
+        @pl.when(jnp.logical_not(jnp.logical_and(bottom, jnp.logical_and(indirect, even))))
+        def _(s=s):
+            first_copy(s).start()
 
     def tile(left, right, slot):
         product = lax.dot_general(
@@ -238,9 +326,11 @@
         tiles[slot + 1] = product[:, CZ:]
 
     def tile_copy(slot):
-        to = slot if slot < 8 else slot - 2
-        where = d if slot < 8 else block(-1)
-        return copy(tiles.at[slot], sums.at[c], tile_send.at[slot], tile_recv.at[c], to, where)
+        if slot < 8:
+            return copy(tiles.at[slot], sums.at[c], tile_send.at[slot], tile_recv.at[c], slot, d)
+        return copy(
+            tiles.at[slot], late_sums.at[c], tile_send.at[slot], late_recv.at[c], slot - 4, block(1)
+        )
 
     def send_tile(slot):
         for q in (slot, slot + 1):
@@ -273,59 +363,104 @@
 
     @pl.when(even)
     def _():
+        for s in range(8):
+            panel_arrived(0, s).wait_recv()
+        tile(PANEL, 0, 2)
+        send_tile(2)
         for j in range(8):
             s = peer(j)
             panel_arrived(1, s).wait_recv()
             passed_copy(s).start()
-        for s in range(8):
-            panel_arrived(0, s).wait_recv()
-        tile(PANEL, 0, 2)
-        send_tile(2)
         tile(PANEL, 1, 4)
         send_tile(4)
+        for s in range(8):
+            panel_arrived(2, s).wait_recv()
+        tile(PANEL, 2, 6)
+        send_tile(6)
+
+        @pl.when(top)
+        def _():
+            tile(0, 2, 8)
+            send_tile(8)
 
     @pl.when(odd == 1)
     def _():
-        for s in range(8):
-            panel_arrived(0, s).wait_recv()
-        tile(0, PANEL, 4)
-        send_tile(4)
+        for j in range(8):
+            s = peer(j)
+            indirect = jnp.logical_and(lax.rem(s, 2) == 1, bottom)
+
+            @pl.when(indirect)
+            def _(s=s):
+                to_relay_copy(s, edge_send).start()
+
+            @pl.when(jnp.logical_not(indirect))
+            def _(s=s):
+                third_copy(s).start()
+
+        @pl.when(inner_bottom)
+        def _():
+            for s in range(8):
+                panel_arrived(0, s).wait_recv()
+            tile(0, PANEL, 4)
+            send_tile(4)
+
         for s in range(8):
             panel_arrived(1, s).wait_recv()
+
+        @pl.when(bottom)
+        def _():
+            tile(PANEL, 1, 2)
+            send_tile(2)
+            for s in range(8):
+                panel_arrived(0, s).wait_recv()
+
         tile(0, 1, 6)
         send_tile(6)
-        tile(PANEL, 1, 2)
-        send_tile(2)
-        for s in range(8):
-            panel_arrived(2, s).wait_recv()
-        tile(2, PANEL, 8)
-        send_tile(8)
-
-    def sum_arrived(s):
-        arrived(sums, tile_recv, s).wait_recv()
-
-    for j in range(1, 8):
-        sum_arrived(peer(j))
-
-    @pl.when(jnp.logical_and(even, c >= 6))
-    def _():
-        sum_arrived(c)
-
-    total = sums[0]
-    for s in range(1, 8):
-        total = total + sums[s]
-    total = total * scale
-
+
+        @pl.when(inner_bottom)
+        def _():
+            tile(PANEL, 1, 2)
+            send_tile(2)
+
+    guest = jnp.logical_not(mine)
+
+    def total(landing):
+        value = landing[0]
+        for s in range(1, 8):
+            value = value + landing[s]
+        return value * scale
+
+    crossing = c >= 6
+    gives = jnp.logical_and(guest, jnp.logical_or(inner_bottom, crossing))
+    takes = jnp.logical_and(guest, jnp.logical_or(inner_top, crossing))
     last = copy(last_out, last_in, last_send, last_recv, c, block(-2))
 
     @pl.when(mine)
     def _():
-        out[...] = total
-
-    @pl.when(jnp.logical_not(mine))
-    def _():
-        last_out[...] = total
+        for j in range(1, 8):
+            arrived(sums, tile_recv, peer(j)).wait_recv()
+        out[...] = total(sums)
+
+    @pl.when(gives)
+    def _():
+        for j in range(1, 8):
+            arrived(sums, tile_recv, peer(j)).wait_recv()
+
+        last_out[...] = total(sums)
         last.start()
+
+    @when(guest, jnp.logical_not(takes))
+    def _():
+        for j in range(1, 8):
+            arrived(late_sums, late_recv, peer(j)).wait_recv()
+
+        arrived(late_sums, late_recv, c).wait_recv()
+        out[...] = total(late_sums)
+
+    @pl.when(takes)
+    def _():
+        last.wait_recv()
+        out[...] = last_in[...]
 
     for j in range(1, 8):
         coef_copy(j).wait_send()
@@ -333,25 +468,39 @@
         out_copy(j).wait_send()
     for s in range(8):
         first_copy(s).wait_send()
-        second_copy(s).wait_send()
     wait_tile(0)
     wait_tile(2)
-    wait_tile(4)
+
+    @when(top)
+    def _():
+        for i in range(4):
+            relayed_copy(i).wait_send()
 
     @pl.when(even)
     def _():
         for s in range(8):
             passed_copy(s).wait_send()
+        wait_tile(4)
+
+        @pl.when(top)
+        def _():
+            wait_tile(8)
 
     @pl.when(odd == 1)
     def _():
-        wait_tile(6)
-        wait_tile(8)
-
-    @pl.when(jnp.logical_not(mine))
-    def _():
-        last.wait()
-        out[...] = last_in[...]
+        for s in range(8):
+            second_copy(s).wait_send()
+            third_copy(s).wait_send()
+
+        @pl.when(inner_bottom)
+        def _():
+            wait_tile(4)
+
+    wait_tile(6)
+
+    @pl.when(gives)
+    def _():
+        last.wait_send()
 
 
 def body(sensitivity, weights, coef_x, coef_y, coef_z):
@@ -375,10 +524,13 @@
             pltpu.VMEM((4, rows, cells), jnp.bfloat16),
             pltpu.VMEM((10, rows, CZ), jnp.float32),
             pltpu.VMEM((8, rows, CZ), jnp.float32),
+            pltpu.VMEM((8, rows, CZ), jnp.float32),
             pltpu.VMEM((rows, CZ), jnp.float32),
             pltpu.VMEM((rows, CZ), jnp.float32),
+            pltpu.VMEM((4, part, cells), jnp.bfloat16),
             dma((7,)), dma((8,)), dma((7,)), dma((8,)), dma((5,)), dma((7,)), dma((8,)),
             dma((8,)), dma((8,)), dma((8,)), dma((3, 8)), dma((10,)), dma((8,)), dma, dma,
+            dma((4,)), dma((4,)), pltpu.SemaphoreType.REGULAR, dma((8,)), dma((8,)),
         ],
         compiler_params=pltpu.CompilerParams(
             collective_id=0, has_side_effects=True, vmem_limit_bytes=60 * 1024 * 1024

time: 75.9 us -> 59.9 us (0.79)
  the two profiles are of different devices: /device:TPU:6 before, /device:TPU:15 now
where the time goes in v3:
time: 59.9 us; the launch traced here: 59.7 us
  Pallas kernels  58.1 us (97%)
  local copies, waits for them, and re-layouts  1.57 us (3%)
    pallas_call x1, Pallas kernels, body(): pl.pallas_call(functools.partial(kernel, scale), out_shape=jax.ShapeDtype...  58.1 us
    unnamed x1, local copies, waits for them, and re-layouts  1.57 us

profile of v3, /device:TPU:15, one launch (start us, length us, event | category | flops | bytes accessed | tf_op | source)
XLA Modules:
  0.0 59.7 jit_solution(11689922102130510310)
XLA Ops:
  0.0 58.1 %gram_band.1 = f32[256,128]{1,0:T(8,128)} custom-call(bf16[256,1024]{1,0:T(8,128)(2,1)} %sens.1, f32[2,128]{1,0:T(2,128)} %bitcast.7, f32[8,128]{1,0:T(8,128)} %bitcast.4, f32[8,128]{1,0:T(8,128)} %bitcast.5, f32[8,128]{1,0:T(8,128)} %bitcast.6), custom_call_target="tpu_custom_call" | custom-call | tf_op jit(solution)/shard_map/gram_band/pallas_call | solution.py:512
  58.2 1.6 %copy.7 = f32[256,128]{1,0:T(8,128)} copy(f32[256,128]{1,0:T(8,128)} %gram_band.1) | data formatting | bytes 262144

commit v4 on v3

v4 whole, which is shorter than its diff:
```python
import functools

import jax
import jax.numpy as jnp
from jax import lax
from jax.experimental import pallas as pl
from jax.experimental.pallas import tpu as pltpu
from jax.sharding import PartitionSpec as P

CY = 4
CZ = 128
GROUP = 16
GROUPS = 2
CHUNKS = 4
COLUMN = 16
MESH = pl.DeviceIdType.MESH
PANEL = 3


def smoothing_pass(load, coef, store):
    def step(part, carry):
        current, entering = carry
        for half in range(2):
            if half == 0:
                above = [load(part, CY + y) for y in range(CY)]
            else:
                upper = jnp.minimum(part + 1, 7)
                above = [load(upper, y) for y in range(CY)]
            flux_x = []
            below_y = None
            for y in range(CY):
                row = half * CY + y
                here = current[y]
                flux = coef[part, pl.ds(row, 1), :] * (above[y] - here)
                change = flux - entering[y]
                flux_x.append(flux)
                if y < CY - 1:
                    flux_y = coef[part, pl.ds(8 + row, 1), :] * (current[y + 1] - here)
                    change = change + flux_y
                if y > 0:
                    change = change - below_y
                below_y = flux_y
                flux_z = coef[part, pl.ds(16 + row, 1), :] * (pltpu.roll(here, CZ - 1, 1) - here)
                change = change + (flux_z - pltpu.roll(flux_z, 1, 1))
                store(part, row, here + change)
            current, entering = tuple(above), tuple(flux_x)
        return current, entering

    first = tuple(load(0, y) for y in range(CY))
    zero = tuple(jnp.zeros((GROUP, CZ), jnp.float32) for _ in range(CY))
    lax.fori_loop(0, 8, step, (first, zero), unroll=4)


def kernel(
    scale, sens, weights_hbm, coef_x, coef_y, coef_z, out,
    weights, gathered, coef, slab_in, field, slab_out, panels, tiles, sums, reduced, landing, relay,
    coef_send, coef_recv, in_send, in_recv, own_sem, out_send, out_recv,
    a_send, b_send, c_send, panel_recv, tile_send, tile_recv, last_send, last_recv,
    relay_send, relay_recv, late, edge_send,
):
    c = lax.axis_index("cells")
    d = lax.axis_index("dp")
    blocks = lax.axis_size("dp")
    odd = lax.rem(d, 2)
    even = odd == 0
    height = lax.rem(d, COLUMN) // 2
    bottom, top = height == 0, height == COLUMN // 2 - 1
    inner_bottom, inner_top = jnp.logical_not(bottom), jnp.logical_not(top)
    first_column, last_column = d < COLUMN, d >= blocks - COLUMN
    rows = sens.shape[0] // 8

    def block(offset):
        return lax.rem(d + offset + blocks, blocks)

    def peer(j):
        return lax.rem(c + j, 8)

    def at_rows(index):
        return pl.ds(pl.multiple_of(index * rows, rows), rows)


    def rows_of(group, index):
        start = group * (8 * GROUP) + index * GROUP
        return pl.ds(pl.multiple_of(start, GROUP), GROUP)

    def slab_rows(group):
        return pl.ds(group * GROUP, GROUP)

    barrier = pltpu.get_barrier_semaphore()

    def greet(cells, dp):
        pl.semaphore_signal(barrier, inc=1, device_id=(cells, dp), device_id_type=MESH)

    def when(*conditions):
        return pl.when(functools.reduce(jnp.logical_and, conditions))

    for j in range(1, 8):
        greet(peer(j), d)
    greet(c, d + 1 - 2 * odd)

    @when(odd == 1, c >= 4, c < 6, top)
    def _():
        for j in range(1, 8):
            greet(peer(j), block(-1))

    @when(inner_top)
    def _():
        greet(c, block(2))

        @pl.when(even)
        def _():
            greet(c, block(3))

    @when(inner_top, odd == 1, c >= 4)
    def _():
        for j in range(1, 8):
            greet(peer(j), block(2))

    @when(bottom)
    def _():
        greet(c, block(COLUMN - 2))
        greet(c, block(-2))

        @pl.when(odd == 1)
        def _():
            greet(c, block(-3))
            for q in (6, 7):

                @pl.when(c != q)
                def _(q=q):
                    greet(q, block(-2))

        @when(odd == 1, jnp.logical_not(last_column))
        def _():
            greet(c, block(COLUMN))

        @when(odd == 1, first_column)
        def _():
            greet(c, block(-COLUMN))

    @when(top, even, jnp.logical_not(last_column))
    def _():
        greet(c, block(COLUMN))
        greet(c, block(COLUMN + 1))

    @when(top, first_column)
    def _():
        greet(c, block(-COLUMN - odd))

    own = [
        pltpu.make_async_copy(source, target, own_sem.at[i])
        for i, (source, target) in enumerate(
            [
                (coef_x, gathered.at[c, pl.ds(0, 8), :]),
                (coef_y, gathered.at[c, pl.ds(8, 8), :]),
                (coef_z, gathered.at[c, pl.ds(16, 8), :]),
                (weights_hbm, weights),
            ]
            + [
                (sens.at[rows_of(group, c), :], slab_in.at[c, slab_rows(group), :])
                for group in range(GROUPS)
            ]
        )
    ]
    for one in own:
        one.start()

    def count(*conditions):
        return functools.reduce(jnp.logical_and, conditions).astype(jnp.int32)

    present = 8 + count(odd == 1, inner_bottom) * 4 - count(odd == 1, inner_bottom, c >= 4)
    present += count(top, odd == 1, c >= 6) * 7
    present += count(bottom, odd == 1, jnp.logical_not(first_column))
    present += count(bottom, odd == 1, last_column)
    present += count(even, top) * 2 - count(even, top, c >= 4, c < 6)
    present += count(inner_bottom) * (1 + odd)
    present += count(top) * (3 - odd) + count(top, jnp.logical_not(first_column))
    present += count(top, even, last_column) * 2
    pl.semaphore_wait(barrier, present)

    def answer(dp, cells=c):
        pl.semaphore_signal(late, inc=1, device_id=(cells, dp), device_id_type=MESH)

    @when(odd == 1, inner_bottom)
    def _():
        answer(block(-2))

    @when(top)
    def _():
        answer(block(2 - COLUMN))

        @pl.when(even)
        def _():
            answer(block(2))
            answer(block(3))

        @when(odd == 1, c >= 6)
        def _():
            for j in range(8):
                answer(block(2), peer(j))

    @when(bottom, odd == 1, jnp.logical_not(first_column))
    def _():
        answer(block(-COLUMN))

    @when(top, even, last_column)
    def _():
        answer(block(COLUMN))
        answer(block(COLUMN + 1))

    def copy(source, target, send, recv, cells, dp):
        return pltpu.make_async_remote_copy(
            src_ref=source, dst_ref=target, send_sem=send, recv_sem=recv,
            device_id=(cells, dp), device_id_type=MESH,
        )

    def coef_copy(j):
        return copy(
            gathered.at[c], gathered.at[c], coef_send.at[j - 1], coef_recv.at[c], peer(j), d
        )

    def in_copy(group, j):
        to = peer(j)
        return copy(
            sens.at[rows_of(group, to), :], slab_in.at[c, slab_rows(group), :],
            in_send.at[group, j - 1], in_recv.at[group, c], to, d,
        )

    for one in own[:3]:
        one.wait()
    for j in range(1, 8):
        coef_copy(j).start()
    for group in range(GROUPS):
        for j in range(1, 8):
            in_copy(group, j).start()

    own[3].wait()
    lane = lax.broadcasted_iota(jnp.int32, (GROUP, CZ), 1)
    line = lax.broadcasted_iota(jnp.int32, (GROUP, CZ), 0)
    chosen = lane == line + c * GROUP

    def arrived(buffer, sem, s):
        return copy(buffer.at[s], buffer.at[s], sem.at[s], sem.at[s], c, d)

    for j in range(1, 8):
        arrived(gathered, coef_recv, peer(j)).wait_recv()
    inner = lax.broadcasted_iota(jnp.int32, (8, CZ), 1) < CZ - 1
    for s in range(8):
        if s < 7:
            coef[s, 0:8, :] = gathered[s, 0:8, :]
        else:
            coef[s, 0:4, :] = gathered[s, 0:4, :]
            coef[s, 4:8, :] = jnp.zeros((4, CZ), jnp.float32)
        coef[s, 8:16, :] = gathered[s, 8:16, :]
        coef[s, 16:24, :] = jnp.where(inner, gathered[s, 16:24, :], 0.0)
    def out_copy(group, j):
        to = peer(j)
        return copy(
            slab_out.at[to, slab_rows(group), :], panels.at[PANEL, rows_of(group, c), :],
            out_send.at[group, j - 1], out_recv.at[group, c], to, d,
        )

    for group in range(GROUPS):
        part_rows = slab_rows(group)
        scaled = jnp.sum(
            jnp.where(chosen, weights[group : group + 1, :], 0.0), axis=1, keepdims=True
        )
        own[4 + group].wait()
        for j in range(1, 8):
            landed = slab_in.at[peer(j), part_rows, :]
            sem = in_recv.at[group, peer(j)]
            copy(landed, landed, sem, sem, c, d).wait_recv()

        def load_in(part, tile, part_rows=part_rows):
            return slab_in[part, part_rows, pl.ds(tile * CZ, CZ)].astype(jnp.float32)

        def store_field(part, tile, value, part_rows=part_rows):
            field[part, part_rows, pl.ds(tile * CZ, CZ)] = value

        def load_field(part, tile, part_rows=part_rows):
            return field[part, part_rows, pl.ds(tile * CZ, CZ)]

        def store_out(part, tile, value, part_rows=part_rows, scaled=scaled):
            slab_out[part, part_rows, pl.ds(tile * CZ, CZ)] = (scaled * value).astype(jnp.bfloat16)

        smoothing_pass(load_in, coef, store_field)
        smoothing_pass(load_field, coef, store_out)

        for j in range(1, 8):
            out_copy(group, j).start()
        panels[PANEL, rows_of(group, c), :] = slab_out[c, part_rows, :]

    first_to = jnp.where(even, block(-2), block(-1))
    first_slot = jnp.where(even, 1, 0)
    chunk = 8 * rows // CHUNKS

    def piece(slot, s):
        return panels.at[slot, pl.ds(s * chunk, chunk), :]

    def first_copy(s):
        return copy(
            piece(PANEL, s), piece(first_slot, s), a_send.at[s], panel_recv.at[first_slot, s], c, first_to
        )

    def second_copy(s):
        return copy(piece(PANEL, s), piece(0, s), b_send.at[s], panel_recv.at[0, s], c, block(2))

    relay_to = jnp.where(bottom, block(COLUMN - 2), block(2 - COLUMN))
    relayed_to = jnp.where(bottom, block(COLUMN), block(-COLUMN - odd))
    relayed_slot = jnp.where(bottom, 0, 1 + odd)

    def to_relay_copy(s, send):
        return copy(
            piece(PANEL, s), relay.at[s // 2], send.at[s], relay_recv.at[s // 2], c, relay_to
        )

    def relayed_copy(i):
        s = 2 * i + 1
        return copy(
            relay.at[i], piece(relayed_slot, s), relay_send.at[i], panel_recv.at[relayed_slot, s], c, relayed_to
        )

    def third_copy(s):
        return copy(piece(PANEL, s), piece(2, s), edge_send.at[s], panel_recv.at[2, s], c, block(-3))

    def pass_relayed():
        for i in range(CHUNKS // 2):
            arrived(relay, relay_recv, i).wait_recv()
            relayed_copy(i).start()

    pl.when(top)(pass_relayed)

    awaited = count(odd == 1, inner_top) + count(bottom) * 2
    awaited += count(bottom, odd == 1) * 2 + count(top, first_column)
    awaited += count(bottom, odd == 1, jnp.logical_not(last_column))

    @pl.when(awaited > 0)
    def _():
        pl.semaphore_wait(late, awaited)

    def passed_copy(s):
        return copy(piece(1, s), piece(1, s), c_send.at[s], panel_recv.at[1, s], c, block(1))

    def panel_arrived(slot, s):
        return copy(
            piece(slot, s), piece(slot, s), panel_recv.at[slot, s], panel_recv.at[slot, s], c, d
        )

    for s in range(CHUNKS):
        group, low = s // 2, s % 2 * 4
        for source in range(low, low + 4):

            @pl.when(c != source)
            def _(group=group, source=source):
                landed = panels.at[PANEL, rows_of(group, source), :]
                sem = out_recv.at[group, source]
                copy(landed, landed, sem, sem, c, d).wait_recv()

        indirect = s % 2 == 1

        up_indirect = jnp.logical_and(top, indirect)
        down_indirect = jnp.logical_and(jnp.logical_and(bottom, even), indirect)

        @when(odd == 1, up_indirect)
        def _(s=s):
            to_relay_copy(s, b_send).start()

        @when(odd == 1, jnp.logical_not(up_indirect))
        def _(s=s):
            second_copy(s).start()

        @pl.when(down_indirect)
        def _(s=s):
            to_relay_copy(s, a_send).start()

        @pl.when(jnp.logical_not(down_indirect))
        def _(s=s):
            first_copy(s).start()

    own_rows = at_rows(c)

    def tile_copy(t, j):
        to = peer(j)
        return copy(
            tiles.at[t, at_rows(to), :], sums.at[t, c], tile_send.at[t, j - 1], tile_recv.at[t, c], to, d
        )

    def tile(left, right, t):
        tiles[t] = lax.dot_general(
            panels[left], panels[right], (((1,), (1,)), ((), ())),
            preferred_element_type=jnp.float32,
        )
        for j in range(1, 8):
            tile_copy(t, j).start()
        sums[t, c] = tiles[t, own_rows, :]

    def final_copy(t, half, to, where):
        return copy(
            reduced.at[t, half], landing.at[own_rows, :], last_send.at[t, half], last_recv.at[c], to, where
        )

    def on_each_half(t, k, where, act, keep):
        for half in range(2):
            to = 2 * k + half
            if where is None:

                @pl.when(c != to)
                def _(half=half, to=to):
                    act(final_copy(t, half, to, d))

                @pl.when(c == to)
                def _(half=half):
                    keep(half)

            else:
                act(final_copy(t, half, to, where))

    def reduce(t, k, where=None):
        for j in range(1, 8):
            s = peer(j)
            copy(sums.at[t, s], sums.at[t, s], tile_recv.at[t, s], tile_recv.at[t, s], c, d).wait_recv()
        value = sums[t, 0]
        for s in range(1, 8):
            value = value + sums[t, s]
        value = value * scale
        reduced[t, 0] = value[:, :CZ]
        reduced[t, 1] = value[:, CZ:]

        def keep(half):
            landing[own_rows, :] = reduced[t, half]

        on_each_half(t, k, where, lambda one: one.start(), keep)

    def end(t, k, where=None):
        for j in range(1, 8):
            tile_copy(t, j).wait_send()
        on_each_half(t, k, where, lambda one: one.wait_send(), lambda half: None)

    tile(PANEL, PANEL, 0)

    @pl.when(even)
    def _():
        for s in range(CHUNKS):
            panel_arrived(0, s).wait_recv()
        tile(PANEL, 0, 1)
        for s in range(CHUNKS):
            panel_arrived(1, s).wait_recv()
            passed_copy(s).start()
        tile(PANEL, 1, 2)
        reduce(0, 0)
        reduce(1, 1)
        for s in range(CHUNKS):
            panel_arrived(2, s).wait_recv()
        tile(PANEL, 2, 3)

        @pl.when(top)
        def _():
            tile(0, 2, 4)

        reduce(2, 2)
        reduce(3, 3)

        @pl.when(top)
        def _():
            reduce(4, 2, block(1))

    @pl.when(odd == 1)
    def _():
        for s in range(CHUNKS):
            indirect = jnp.logical_and(s % 2 == 1, bottom)

            @pl.when(indirect)
            def _(s=s):
                to_relay_copy(s, edge_send).start()

            @pl.when(jnp.logical_not(indirect))
            def _(s=s):
                third_copy(s).start()

        @pl.when(inner_bottom)
        def _():
            for s in range(CHUNKS):
                panel_arrived(0, s).wait_recv()
            tile(0, PANEL, 2)

        for s in range(CHUNKS):
            panel_arrived(1, s).wait_recv()

        @pl.when(bottom)
        def _():
            tile(PANEL, 1, 1)
            pass_relayed()
            reduce(0, 0)
            reduce(1, 1)
            for s in range(CHUNKS):
                panel_arrived(0, s).wait_recv()

        tile(0, 1, 3)

        @pl.when(inner_bottom)
        def _():
            tile(PANEL, 1, 1)
            reduce(0, 0)
            reduce(2, 2, block(-2))

        reduce(3, 3, block(-2))

        @pl.when(inner_bottom)
        def _():
            reduce(1, 1)

    for j in range(1, 8):
        copy(
            landing.at[at_rows(peer(j)), :], landing.at[at_rows(peer(j)), :],
            last_recv.at[peer(j)], last_recv.at[peer(j)], c, d,
        ).wait_recv()

    @when(odd == 1, c >= 4)
    def _():
        copy(
            landing.at[own_rows, :], landing.at[own_rows, :], last_recv.at[c], last_recv.at[c], c, d
        ).wait_recv()

    out[...] = landing[...]

    for j in range(1, 8):
        coef_copy(j).wait_send()
        for group in range(GROUPS):
            in_copy(group, j).wait_send()
            out_copy(group, j).wait_send()
    for s in range(CHUNKS):
        first_copy(s).wait_send()
    end(0, 0)
    end(1, 1)

    @pl.when(jnp.logical_or(top, jnp.logical_and(bottom, odd == 1)))
    def _():
        for i in range(CHUNKS // 2):
            relayed_copy(i).wait_send()

    @pl.when(even)
    def _():
        for s in range(CHUNKS):
            passed_copy(s).wait_send()
        end(2, 2)
        end(3, 3)

        @pl.when(top)
        def _():
            end(4, 2, block(1))

    @pl.when(odd == 1)
    def _():
        for s in range(CHUNKS):
            second_copy(s).wait_send()
            third_copy(s).wait_send()

        @pl.when(inner_bottom)
        def _():
            end(2, 2, block(-2))

        end(3, 3, block(-2))


def body(sensitivity, weights, coef_x, coef_y, coef_z):
    rows, cells = sensitivity.shape
    part = rows // 8
    scale = float(cells * lax.axis_size("cells")) ** (-0.5)
    vmem = pl.BlockSpec(memory_space=pltpu.VMEM)
    dma = pltpu.SemaphoreType.DMA
    return pl.pallas_call(
        functools.partial(kernel, scale),
        out_shape=jax.ShapeDtypeStruct((rows, rows // 2), jnp.float32),
        in_specs=[pl.BlockSpec(memory_space=pl.ANY)] * 5,
        out_specs=vmem,
        scratch_shapes=[
            pltpu.VMEM((2, CZ), jnp.float32),
            pltpu.VMEM((8, 24, CZ), jnp.float32),
            pltpu.VMEM((8, 24, CZ), jnp.float32),
            pltpu.VMEM((8, part, cells), jnp.bfloat16),
            pltpu.VMEM((8, part, cells), jnp.float32),
            pltpu.VMEM((8, part, cells), jnp.bfloat16),
            pltpu.VMEM((4, rows, cells), jnp.bfloat16),
            pltpu.VMEM((5, rows, rows), jnp.float32),
            pltpu.VMEM((5, 8, part, rows), jnp.float32),
            pltpu.VMEM((5, 2, part, CZ), jnp.float32),
            pltpu.VMEM((rows, CZ), jnp.float32),
            pltpu.VMEM((CHUNKS // 2, rows // CHUNKS, cells), jnp.bfloat16),
            dma((7,)), dma((8,)), dma((GROUPS, 7)), dma((GROUPS, 8)), dma((4 + GROUPS,)), dma((GROUPS, 7)), dma((GROUPS, 8)),
            dma((CHUNKS,)), dma((CHUNKS,)), dma((CHUNKS,)), dma((3, CHUNKS)), dma((5, 7)), dma((5, 8)), dma((5, 2)), dma((8,)),
            dma((CHUNKS // 2,)), dma((CHUNKS // 2,)), pltpu.SemaphoreType.REGULAR, dma((CHUNKS,)),
        ],
        compiler_params=pltpu.CompilerParams(
            collective_id=0, has_side_effects=True, vmem_limit_bytes=60 * 1024 * 1024
        ),
        name="gram_band",
    )(
        sensitivity,
        weights.reshape(2, CZ),
        coef_x.reshape(8, CZ),
        coef_y.reshape(8, CZ),
        coef_z.reshape(8, CZ),
    )


def solution(mesh):
    return jax.shard_map(
        body,
        mesh=mesh,
        in_specs=(P("dp", "cells"), P("dp"), P("cells"), P("cells"), P("cells")),
        out_specs=P("dp", "cells"),
        check_vma=False,
    )
```

time: 59.9 us -> 58.9 us (0.983)
  the two profiles are of different devices: /device:TPU:15 before, /device:TPU:1 now
where the time goes in v4:
time: 58.9 us; the launch traced here: 58.7 us
  Pallas kernels  57.1 us (97%)
  local copies, waits for them, and re-layouts  1.57 us (3%)
    pallas_call x1, Pallas kernels, body(): pl.pallas_call(functools.partial(kernel, scale), out_shape=jax.ShapeDtype...  57.1 us
    unnamed x1, local copies, waits for them, and re-layouts  1.57 us

profile of v4, /device:TPU:1, one launch (start us, length us, event | category | flops | bytes accessed | tf_op | source)
XLA Modules:
  0.0 58.7 jit_solution(14782014712117289298)
XLA Ops:
  0.0 57.1 %gram_band.1 = f32[256,128]{1,0:T(8,128)} custom-call(bf16[256,1024]{1,0:T(8,128)(2,1)} %sens.1, f32[2,128]{1,0:T(2,128)} %bitcast.7, f32[8,128]{1,0:T(8,128)} %bitcast.4, f32[8,128]{1,0:T(8,128)} %bitcast.5, f32[8,128]{1,0:T(8,128)} %bitcast.6), custom_call_target="tpu_custom_call" | custom-call | tf_op jit(solution)/shard_map/gram_band/pallas_call | solution.py:571
  57.1 1.6 %copy.7 = f32[256,128]{1,0:T(8,128)} copy(f32[256,128]{1,0:T(8,128)} %gram_band.1) | data formatting | bytes 262144

commit v5 on v4

--- a/solution.py
+++ b/solution.py
@@ -53,10 +53,10 @@
 
 def kernel(
     scale, sens, weights_hbm, coef_x, coef_y, coef_z, out,
-    weights, gathered, coef, slab_in, field, slab_out, panels, tiles, sums, reduced, landing, relay,
+    weights, gathered, coef, slab_in, field, slab_out, panels, tiles, sums, reduced, landing, far, relay,
     coef_send, coef_recv, in_send, in_recv, own_sem, out_send, out_recv,
     a_send, b_send, c_send, panel_recv, tile_send, tile_recv, last_send, last_recv,
-    relay_send, relay_recv, late, edge_send,
+    relay_send, relay_recv, late, edge_send, far_recv,
 ):
     c = lax.axis_index("cells")
     d = lax.axis_index("dp")
@@ -130,13 +130,6 @@
                 def _(q=q):
                     greet(q, block(-2))
 
-        @when(odd == 1, jnp.logical_not(last_column))
-        def _():
-            greet(c, block(COLUMN))
-
-        @when(odd == 1, first_column)
-        def _():
-            greet(c, block(-COLUMN))
 
     @when(top, even, jnp.logical_not(last_column))
     def _():
@@ -170,8 +163,6 @@
 
     present = 8 + count(odd == 1, inner_bottom) * 4 - count(odd == 1, inner_bottom, c >= 4)
     present += count(top, odd == 1, c >= 6) * 7
-    present += count(bottom, odd == 1, jnp.logical_not(first_column))
-    present += count(bottom, odd == 1, last_column)
     present += count(even, top) * 2 - count(even, top, c >= 4, c < 6)
     present += count(inner_bottom) * (1 + odd)
     present += count(top) * (3 - odd) + count(top, jnp.logical_not(first_column))
@@ -198,10 +189,6 @@
         def _():
             for j in range(8):
                 answer(block(2), peer(j))
-
-    @when(bottom, odd == 1, jnp.logical_not(first_column))
-    def _():
-        answer(block(-COLUMN))
 
     @when(top, even, last_column)
     def _():
@@ -305,34 +292,31 @@
     def second_copy(s):
         return copy(piece(PANEL, s), piece(0, s), b_send.at[s], panel_recv.at[0, s], c, block(2))
 
-    relay_to = jnp.where(bottom, block(COLUMN - 2), block(2 - COLUMN))
-    relayed_to = jnp.where(bottom, block(COLUMN), block(-COLUMN - odd))
-    relayed_slot = jnp.where(bottom, 0, 1 + odd)
+    relayed_slot = 1 + odd
 
     def to_relay_copy(s, send):
         return copy(
-            piece(PANEL, s), relay.at[s // 2], send.at[s], relay_recv.at[s // 2], c, relay_to
+            piece(PANEL, s), relay.at[s // 2], send.at[s], relay_recv.at[s // 2], c, block(COLUMN - 2)
         )
 
     def relayed_copy(i):
         s = 2 * i + 1
         return copy(
-            relay.at[i], piece(relayed_slot, s), relay_send.at[i], panel_recv.at[relayed_slot, s], c, relayed_to
+            relay.at[i], piece(relayed_slot, s), relay_send.at[i], panel_recv.at[relayed_slot, s], c, block(-COLUMN - odd)
         )
 
     def third_copy(s):
         return copy(piece(PANEL, s), piece(2, s), edge_send.at[s], panel_recv.at[2, s], c, block(-3))
 
-    def pass_relayed():
-        for i in range(CHUNKS // 2):
+    def pass_relayed(first=0):
+        for i in range(first, CHUNKS // 2):
             arrived(relay, relay_recv, i).wait_recv()
             relayed_copy(i).start()
 
-    pl.when(top)(pass_relayed)
+    pl.when(jnp.logical_and(top, even))(pass_relayed)
 
     awaited = count(odd == 1, inner_top) + count(bottom) * 2
     awaited += count(bottom, odd == 1) * 2 + count(top, first_column)
-    awaited += count(bottom, odd == 1, jnp.logical_not(last_column))
 
     @pl.when(awaited > 0)
     def _():
@@ -358,14 +342,9 @@
 
         indirect = s % 2 == 1
 
-        up_indirect = jnp.logical_and(top, indirect)
         down_indirect = jnp.logical_and(jnp.logical_and(bottom, even), indirect)
 
-        @when(odd == 1, up_indirect)
-        def _(s=s):
-            to_relay_copy(s, b_send).start()
-
-        @when(odd == 1, jnp.logical_not(up_indirect))
+        @pl.when(odd == 1)
         def _(s=s):
             second_copy(s).start()
 
@@ -385,11 +364,19 @@
             tiles.at[t, at_rows(to), :], sums.at[t, c], tile_send.at[t, j - 1], tile_recv.at[t, c], to, d
         )
 
-    def tile(left, right, t):
+    def form(left, right, t):
         tiles[t] = lax.dot_general(
             panels[left], panels[right], (((1,), (1,)), ((), ())),
             preferred_element_type=jnp.float32,
         )
+
+    def far_copy(half):
+        return copy(
+            tiles.at[3, :, pl.ds(half * CZ, CZ)], far.at[c], last_send.at[3, half], far_recv.at[c], 6 + half, block(-2)
+        )
+
+    def tile(left, right, t):
+        form(left, right, t)
         for j in range(1, 8):
             tile_copy(t, j).start()
         sums[t, c] = tiles[t, own_rows, :]
@@ -467,7 +454,7 @@
     @pl.when(odd == 1)
     def _():
         for s in range(CHUNKS):
-            indirect = jnp.logical_and(s % 2 == 1, bottom)
+            indirect = jnp.logical_and(s == CHUNKS - 1, bottom)
 
             @pl.when(indirect)
             def _(s=s):
@@ -477,6 +464,8 @@
             def _(s=s):
                 third_copy(s).start()
 
+        pl.when(top)(functools.partial(pass_relayed, CHUNKS // 2 - 1))
+
         @pl.when(inner_bottom)
         def _():
             for s in range(CHUNKS):
@@ -489,39 +478,48 @@
         @pl.when(bottom)
         def _():
             tile(PANEL, 1, 1)
-            pass_relayed()
             reduce(0, 0)
             reduce(1, 1)
             for s in range(CHUNKS):
                 panel_arrived(0, s).wait_recv()
-
-        tile(0, 1, 3)
+            form(0, 1, 3)
+            for half in range(2):
+                far_copy(half).start()
 
         @pl.when(inner_bottom)
         def _():
             tile(PANEL, 1, 1)
+            tile(0, 1, 3)
             reduce(0, 0)
             reduce(2, 2, block(-2))
-
-        reduce(3, 3, block(-2))
-
-        @pl.when(inner_bottom)
-        def _():
             reduce(1, 1)
-
-    for j in range(1, 8):
-        copy(
-            landing.at[at_rows(peer(j)), :], landing.at[at_rows(peer(j)), :],
-            last_recv.at[peer(j)], last_recv.at[peer(j)], c, d,
-        ).wait_recv()
-
-    @when(odd == 1, c >= 4)
-    def _():
-        copy(
-            landing.at[own_rows, :], landing.at[own_rows, :], last_recv.at[c], last_recv.at[c], c, d
-        ).wait_recv()
-
-    out[...] = landing[...]
+            reduce(3, 3, block(-2))
+
+    from_far = functools.reduce(jnp.logical_and, [top, odd == 1, c >= 6])
+
+    @pl.when(from_far)
+    def _():
+        for s in range(8):
+            arrived(far, far_recv, s).wait_recv()
+        value = far[0]
+        for s in range(1, 8):
+            value = value + far[s]
+        out[...] = value * scale
+
+    @pl.when(jnp.logical_not(from_far))
+    def _():
+        def landed(s):
+            part = landing.at[at_rows(s), :]
+            return copy(part, part, last_recv.at[s], last_recv.at[s], c, d)
+
+        for j in range(1, 8):
+            landed(peer(j)).wait_recv()
+
+        @when(odd == 1, c >= 4)
+        def _():
+            landed(c).wait_recv()
+
+        out[...] = landing[...]
 
     for j in range(1, 8):
         coef_copy(j).wait_send()
@@ -533,10 +531,14 @@
     end(0, 0)
     end(1, 1)
 
-    @pl.when(jnp.logical_or(top, jnp.logical_and(bottom, odd == 1)))
-    def _():
-        for i in range(CHUNKS // 2):
-            relayed_copy(i).wait_send()
+    @when(top)
+    def _():
+        relayed_copy(CHUNKS // 2 - 1).wait_send()
+
+        @pl.when(even)
+        def _():
+            for i in range(CHUNKS // 2 - 1):
+                relayed_copy(i).wait_send()
 
     @pl.when(even)
     def _():
@@ -558,8 +560,12 @@
         @pl.when(inner_bottom)
         def _():
             end(2, 2, block(-2))
-
-        end(3, 3, block(-2))
+            end(3, 3, block(-2))
+
+        @pl.when(bottom)
+        def _():
+            for half in range(2):
+                far_copy(half).wait_send()
 
 
 def body(sensitivity, weights, coef_x, coef_y, coef_z):
@@ -585,10 +591,11 @@
             pltpu.VMEM((5, 8, part, rows), jnp.float32),
             pltpu.VMEM((5, 2, part, CZ), jnp.float32),
             pltpu.VMEM((rows, CZ), jnp.float32),
+            pltpu.VMEM((8, rows, CZ), jnp.float32),
             pltpu.VMEM((CHUNKS // 2, rows // CHUNKS, cells), jnp.bfloat16),
             dma((7,)), dma((8,)), dma((GROUPS, 7)), dma((GROUPS, 8)), dma((4 + GROUPS,)), dma((GROUPS, 7)), dma((GROUPS, 8)),
             dma((CHUNKS,)), dma((CHUNKS,)), dma((CHUNKS,)), dma((3, CHUNKS)), dma((5, 7)), dma((5, 8)), dma((5, 2)), dma((8,)),
-            dma((CHUNKS // 2,)), dma((CHUNKS // 2,)), pltpu.SemaphoreType.REGULAR, dma((CHUNKS,)),
+            dma((CHUNKS // 2,)), dma((CHUNKS // 2,)), pltpu.SemaphoreType.REGULAR, dma((CHUNKS,)), dma((8,)),
         ],
         compiler_params=pltpu.CompilerParams(
             collective_id=0, has_side_effects=True, vmem_limit_bytes=60 * 1024 * 1024

time: 58.9 us -> 57 us (0.968)
  Pallas kernels: 57.1 us -> 54.7 us
    pallas_call x1, Pallas kernels: 57.1 us -> 54.7 us  [body(): pl.pallas_call(functools.partial(kernel, scale), out_shape=jax.ShapeDtype...]
where the time goes in v5:
time: 57 us; the launch traced here: 56.3 us
  Pallas kernels  54.7 us (96%)
  local copies, waits for them, and re-layouts  1.57 us (3%)
    pallas_call x1, Pallas kernels, body(): pl.pallas_call(functools.partial(kernel, scale), out_shape=jax.ShapeDtype...  54.7 us
    unnamed x1, local copies, waits for them, and re-layouts  1.57 us

profile of v5, /device:TPU:1, one launch (start us, length us, event | category | flops | bytes accessed | tf_op | source)
XLA Modules:
  0.0 56.3 jit_solution(16625011452251667867)
XLA Ops:
  0.0 54.7 %gram_band.1 = f32[256,128]{1,0:T(8,128)} custom-call(bf16[256,1024]{1,0:T(8,128)(2,1)} %sens.1, f32[2,128]{1,0:T(2,128)} %bitcast.7, f32[8,128]{1,0:T(8,128)} %bitcast.4, f32[8,128]{1,0:T(8,128)} %bitcast.5, f32[8,128]{1,0:T(8,128)} %bitcast.6), custom_call_target="tpu_custom_call" | custom-call | tf_op jit(solution)/shard_map/gram_band/pallas_call | solution.py:577
  54.7 1.6 %copy.7 = f32[256,128]{1,0:T(8,128)} copy(f32[256,128]{1,0:T(8,128)} %gram_band.1) | data formatting | bytes 262144

commit v6 on v5

--- a/solution.py
+++ b/solution.py
@@ -56,7 +56,7 @@
     weights, gathered, coef, slab_in, field, slab_out, panels, tiles, sums, reduced, landing, far, relay,
     coef_send, coef_recv, in_send, in_recv, own_sem, out_send, out_recv,
     a_send, b_send, c_send, panel_recv, tile_send, tile_recv, last_send, last_recv,
-    relay_send, relay_recv, late, edge_send, far_recv,
+    relay_send, relay_recv, late, edge_send, far_recv, far_send,
 ):
     c = lax.axis_index("cells")
     d = lax.axis_index("dp")
@@ -370,10 +370,15 @@
             preferred_element_type=jnp.float32,
         )
 
-    def far_copy(half):
-        return copy(
-            tiles.at[3, :, pl.ds(half * CZ, CZ)], far.at[c], last_send.at[3, half], far_recv.at[c], 6 + half, block(-2)
-        )
+    def far_copy(t, half, first, where):
+        return copy(
+            tiles.at[t, :, pl.ds(half * CZ, CZ)], far.at[c], far_send.at[half], far_recv.at[c], first + half, where
+        )
+
+    def far_tile(left, right, t, first, where):
+        form(left, right, t)
+        for half in range(2):
+            far_copy(t, half, first, where).start()
 
     def tile(left, right, t):
         form(left, right, t)
@@ -442,14 +447,10 @@
 
         @pl.when(top)
         def _():
-            tile(0, 2, 4)
+            far_tile(0, 2, 4, 4, block(1))
 
         reduce(2, 2)
         reduce(3, 3)
-
-        @pl.when(top)
-        def _():
-            reduce(4, 2, block(1))
 
     @pl.when(odd == 1)
     def _():
@@ -482,9 +483,7 @@
             reduce(1, 1)
             for s in range(CHUNKS):
                 panel_arrived(0, s).wait_recv()
-            form(0, 1, 3)
-            for half in range(2):
-                far_copy(half).start()
+            far_tile(0, 1, 3, 6, block(-2))
 
         @pl.when(inner_bottom)
         def _():
@@ -495,7 +494,7 @@
             reduce(1, 1)
             reduce(3, 3, block(-2))
 
-    from_far = functools.reduce(jnp.logical_and, [top, odd == 1, c >= 6])
+    from_far = functools.reduce(jnp.logical_and, [top, odd == 1, c >= 4])
 
     @pl.when(from_far)
     def _():
@@ -549,7 +548,8 @@
 
         @pl.when(top)
         def _():
-            end(4, 2, block(1))
+            for half in range(2):
+                far_copy(4, half, 4, block(1)).wait_send()
 
     @pl.when(odd == 1)
     def _():
@@ -565,7 +565,7 @@
         @pl.when(bottom)
         def _():
             for half in range(2):
-                far_copy(half).wait_send()
+                far_copy(3, half, 6, block(-2)).wait_send()
 
 
 def body(sensitivity, weights, coef_x, coef_y, coef_z):
@@ -588,14 +588,14 @@
             pltpu.VMEM((8, part, cells), jnp.bfloat16),
             pltpu.VMEM((4, rows, cells), jnp.bfloat16),
             pltpu.VMEM((5, rows, rows), jnp.float32),
-            pltpu.VMEM((5, 8, part, rows), jnp.float32),
-            pltpu.VMEM((5, 2, part, CZ), jnp.float32),
+            pltpu.VMEM((4, 8, part, rows), jnp.float32),
+            pltpu.VMEM((4, 2, part, CZ), jnp.float32),
             pltpu.VMEM((rows, CZ), jnp.float32),
             pltpu.VMEM((8, rows, CZ), jnp.float32),
             pltpu.VMEM((CHUNKS // 2, rows // CHUNKS, cells), jnp.bfloat16),
             dma((7,)), dma((8,)), dma((GROUPS, 7)), dma((GROUPS, 8)), dma((4 + GROUPS,)), dma((GROUPS, 7)), dma((GROUPS, 8)),
-            dma((CHUNKS,)), dma((CHUNKS,)), dma((CHUNKS,)), dma((3, CHUNKS)), dma((5, 7)), dma((5, 8)), dma((5, 2)), dma((8,)),
-            dma((CHUNKS // 2,)), dma((CHUNKS // 2,)), pltpu.SemaphoreType.REGULAR, dma((CHUNKS,)), dma((8,)),
+            dma((CHUNKS,)), dma((CHUNKS,)), dma((CHUNKS,)), dma((3, CHUNKS)), dma((4, 7)), dma((4, 8)), dma((4, 2)), dma((8,)),
+            dma((CHUNKS // 2,)), dma((CHUNKS // 2,)), pltpu.SemaphoreType.REGULAR, dma((CHUNKS,)), dma((8,)), dma((2,)),
         ],
         compiler_params=pltpu.CompilerParams(
             collective_id=0, has_side_effects=True, vmem_limit_bytes=60 * 1024 * 1024

time: 57 us -> 56.3 us (0.988)
  no operation moved by 1% of the time
where the time goes in v6:
time: 56.3 us; the launch traced here: 56.2 us
  Pallas kernels  54.6 us (97%)
  local copies, waits for them, and re-layouts  1.57 us (3%)
    pallas_call x1, Pallas kernels, body(): pl.pallas_call(functools.partial(kernel, scale), out_shape=jax.ShapeDtype...  54.6 us
    unnamed x1, local copies, waits for them, and re-layouts  1.57 us

profile of v6, /device:TPU:1, one launch (start us, length us, event | category | flops | bytes accessed | tf_op | source)
XLA Modules:
  0.0 56.2 jit_solution(6823512924977623580)
XLA Ops:
  0.0 54.6 %gram_band.1 = f32[256,128]{1,0:T(8,128)} custom-call(bf16[256,1024]{1,0:T(8,128)(2,1)} %sens.1, f32[2,128]{1,0:T(2,128)} %bitcast.7, f32[8,128]{1,0:T(8,128)} %bitcast.4, f32[8,128]{1,0:T(8,128)} %bitcast.5, f32[8,128]{1,0:T(8,128)} %bitcast.6), custom_call_target="tpu_custom_call" | custom-call | tf_op jit(solution)/shard_map/gram_band/pallas_call | solution.py:577
  54.6 1.6 %copy.7 = f32[256,128]{1,0:T(8,128)} copy(f32[256,128]{1,0:T(8,128)} %gram_band.1) | data formatting | bytes 262144

commit v7 on v6

--- a/solution.py
+++ b/solution.py
@@ -56,7 +56,7 @@
     weights, gathered, coef, slab_in, field, slab_out, panels, tiles, sums, reduced, landing, far, relay,
     coef_send, coef_recv, in_send, in_recv, own_sem, out_send, out_recv,
     a_send, b_send, c_send, panel_recv, tile_send, tile_recv, last_send, last_recv,
-    relay_send, relay_recv, late, edge_send, far_recv, far_send,
+    relay_send, relay_recv, late, edge_send, far_recv, far_send, across_send,
 ):
     c = lax.axis_index("cells")
     d = lax.axis_index("dp")
@@ -124,11 +124,12 @@
         @pl.when(odd == 1)
         def _():
             greet(c, block(-3))
-            for q in (6, 7):
-
-                @pl.when(c != q)
-                def _(q=q):
-                    greet(q, block(-2))
+            for j in range(1, 8):
+                greet(peer(j), block(-2))
+
+        @when(odd == 1, jnp.logical_not(last_column))
+        def _():
+            greet(c, block(COLUMN))
 
 
     @when(top, even, jnp.logical_not(last_column))
@@ -162,7 +163,8 @@
         return functools.reduce(jnp.logical_and, conditions).astype(jnp.int32)
 
     present = 8 + count(odd == 1, inner_bottom) * 4 - count(odd == 1, inner_bottom, c >= 4)
-    present += count(top, odd == 1, c >= 6) * 7
+    present += count(top, odd == 1) * 7
+    present += count(bottom, odd == 1, jnp.logical_not(first_column))
     present += count(even, top) * 2 - count(even, top, c >= 4, c < 6)
     present += count(inner_bottom) * (1 + odd)
     present += count(top) * (3 - odd) + count(top, jnp.logical_not(first_column))
@@ -185,10 +187,14 @@
             answer(block(2))
             answer(block(3))
 
-        @when(odd == 1, c >= 6)
+        @pl.when(odd == 1)
         def _():
             for j in range(8):
                 answer(block(2), peer(j))
+
+    @when(bottom, odd == 1, jnp.logical_not(first_column))
+    def _():
+        answer(block(-COLUMN))
 
     @when(top, even, last_column)
     def _():
@@ -292,17 +298,19 @@
     def second_copy(s):
         return copy(piece(PANEL, s), piece(0, s), b_send.at[s], panel_recv.at[0, s], c, block(2))
 
-    relayed_slot = 1 + odd
+    relay_to = jnp.where(bottom, block(COLUMN - 2), block(2 - COLUMN))
+    relayed_to = jnp.where(bottom, block(COLUMN), block(-COLUMN - odd))
+    relayed_slot = jnp.where(bottom, 0, 1 + odd)
 
     def to_relay_copy(s, send):
         return copy(
-            piece(PANEL, s), relay.at[s // 2], send.at[s], relay_recv.at[s // 2], c, block(COLUMN - 2)
+            piece(PANEL, s), relay.at[s // 2], send.at[s], relay_recv.at[s // 2], c, relay_to
         )
 
     def relayed_copy(i):
         s = 2 * i + 1
         return copy(
-            relay.at[i], piece(relayed_slot, s), relay_send.at[i], panel_recv.at[relayed_slot, s], c, block(-COLUMN - odd)
+            relay.at[i], piece(relayed_slot, s), relay_send.at[i], panel_recv.at[relayed_slot, s], c, relayed_to
         )
 
     def third_copy(s):
@@ -316,7 +324,8 @@
     pl.when(jnp.logical_and(top, even))(pass_relayed)
 
     awaited = count(odd == 1, inner_top) + count(bottom) * 2
-    awaited += count(bottom, odd == 1) * 2 + count(top, first_column)
+    awaited += count(bottom, odd == 1) * 8 + count(top, first_column)
+    awaited += count(bottom, odd == 1, jnp.logical_not(last_column))
 
     @pl.when(awaited > 0)
     def _():
@@ -344,7 +353,13 @@
 
         down_indirect = jnp.logical_and(jnp.logical_and(bottom, even), indirect)
 
-        @pl.when(odd == 1)
+        up_indirect = functools.reduce(jnp.logical_and, [top, indirect, jnp.logical_not(last_column)])
+
+        @when(odd == 1, up_indirect)
+        def _(s=s):
+            to_relay_copy(s, b_send).start()
+
+        @when(odd == 1, jnp.logical_not(up_indirect))
         def _(s=s):
             second_copy(s).start()
 
@@ -380,6 +395,12 @@
         for half in range(2):
             far_copy(t, half, first, where).start()
 
+    def across_copy(j):
+        to = peer(j)
+        return copy(
+            tiles.at[3, at_rows(to), :], sums.at[4, c], across_send.at[j], tile_recv.at[4, c], to, block(-2)
+        )
+
     def tile(left, right, t):
         form(left, right, t)
         for j in range(1, 8):
@@ -407,8 +428,8 @@
             else:
                 act(final_copy(t, half, to, where))
 
-    def reduce(t, k, where=None):
-        for j in range(1, 8):
+    def reduce(t, k, where=None, first=1):
+        for j in range(first, 8):
             s = peer(j)
             copy(sums.at[t, s], sums.at[t, s], tile_recv.at[t, s], tile_recv.at[t, s], c, d).wait_recv()
         value = sums[t, 0]
@@ -427,6 +448,19 @@
         for j in range(1, 8):
             tile_copy(t, j).wait_send()
         on_each_half(t, k, where, lambda one: one.wait_send(), lambda half: None)
+
+    @pl.when(odd == 1)
+    def _():
+        for s in range(CHUNKS):
+            indirect = jnp.logical_and(s == CHUNKS - 1, bottom)
+
+            @pl.when(indirect)
+            def _(s=s):
+                to_relay_copy(s, edge_send).start()
+
+            @pl.when(jnp.logical_not(indirect))
+            def _(s=s):
+                third_copy(s).start()
 
     tile(PANEL, PANEL, 0)
 
@@ -454,16 +488,6 @@
 
     @pl.when(odd == 1)
     def _():
-        for s in range(CHUNKS):
-            indirect = jnp.logical_and(s == CHUNKS - 1, bottom)
-
-            @pl.when(indirect)
-            def _(s=s):
-                to_relay_copy(s, edge_send).start()
-
-            @pl.when(jnp.logical_not(indirect))
-            def _(s=s):
-                third_copy(s).start()
 
         pl.when(top)(functools.partial(pass_relayed, CHUNKS // 2 - 1))
 
@@ -479,11 +503,14 @@
         @pl.when(bottom)
         def _():
             tile(PANEL, 1, 1)
+            pl.when(jnp.logical_not(last_column))(pass_relayed)
             reduce(0, 0)
             reduce(1, 1)
             for s in range(CHUNKS):
                 panel_arrived(0, s).wait_recv()
-            far_tile(0, 1, 3, 6, block(-2))
+            form(0, 1, 3)
+            for j in range(8):
+                across_copy(j).start()
 
         @pl.when(inner_bottom)
         def _():
@@ -494,7 +521,11 @@
             reduce(1, 1)
             reduce(3, 3, block(-2))
 
-    from_far = functools.reduce(jnp.logical_and, [top, odd == 1, c >= 4])
+        @pl.when(top)
+        def _():
+            reduce(4, 3, first=0)
+
+    from_far = functools.reduce(jnp.logical_and, [top, odd == 1, c >= 4, c < 6])
 
     @pl.when(from_far)
     def _():
@@ -514,7 +545,7 @@
         for j in range(1, 8):
             landed(peer(j)).wait_recv()
 
-        @when(odd == 1, c >= 4)
+        @when(odd == 1, c >= 4, inner_top)
         def _():
             landed(c).wait_recv()
 
@@ -530,6 +561,11 @@
     end(0, 0)
     end(1, 1)
 
+    @when(bottom, odd == 1, jnp.logical_not(last_column))
+    def _():
+        for i in range(CHUNKS // 2):
+            relayed_copy(i).wait_send()
+
     @when(top)
     def _():
         relayed_copy(CHUNKS // 2 - 1).wait_send()
@@ -564,8 +600,12 @@
 
         @pl.when(bottom)
         def _():
-            for half in range(2):
-                far_copy(3, half, 6, block(-2)).wait_send()
+            for j in range(8):
+                across_copy(j).wait_send()
+
+        @pl.when(top)
+        def _():
+            on_each_half(4, 3, None, lambda one: one.wait_send(), lambda half: None)
 
 
 def body(sensitivity, weights, coef_x, coef_y, coef_z):
@@ -588,14 +628,14 @@
             pltpu.VMEM((8, part, cells), jnp.bfloat16),
             pltpu.VMEM((4, rows, cells), jnp.bfloat16),
             pltpu.VMEM((5, rows, rows), jnp.float32),
-            pltpu.VMEM((4, 8, part, rows), jnp.float32),
-            pltpu.VMEM((4, 2, part, CZ), jnp.float32),
+            pltpu.VMEM((5, 8, part, rows), jnp.float32),
+            pltpu.VMEM((5, 2, part, CZ), jnp.float32),
             pltpu.VMEM((rows, CZ), jnp.float32),
             pltpu.VMEM((8, rows, CZ), jnp.float32),
             pltpu.VMEM((CHUNKS // 2, rows // CHUNKS, cells), jnp.bfloat16),
             dma((7,)), dma((8,)), dma((GROUPS, 7)), dma((GROUPS, 8)), dma((4 + GROUPS,)), dma((GROUPS, 7)), dma((GROUPS, 8)),
-            dma((CHUNKS,)), dma((CHUNKS,)), dma((CHUNKS,)), dma((3, CHUNKS)), dma((4, 7)), dma((4, 8)), dma((4, 2)), dma((8,)),
-            dma((CHUNKS // 2,)), dma((CHUNKS // 2,)), pltpu.SemaphoreType.REGULAR, dma((CHUNKS,)), dma((8,)), dma((2,)),
+            dma((CHUNKS,)), dma((CHUNKS,)), dma((CHUNKS,)), dma((3, CHUNKS)), dma((4, 7)), dma((5, 8)), dma((5, 2)), dma((8,)),
+            dma((CHUNKS // 2,)), dma((CHUNKS // 2,)), pltpu.SemaphoreType.REGULAR, dma((CHUNKS,)), dma((8,)), dma((2,)), dma((8,)),
         ],
         compiler_params=pltpu.CompilerParams(
             collective_id=0, has_side_effects=True, vmem_limit_bytes=60 * 1024 * 1024

time: 56.3 us -> 55 us (0.977)
  Pallas kernels: 54.6 us -> 53.2 us
    pallas_call x1, Pallas kernels: 54.6 us -> 53.2 us  [body(): pl.pallas_call(functools.partial(kernel, scale), out_shape=jax.ShapeDtype...]
where the time goes in v7:
time: 55 us; the launch traced here: 54.8 us
  Pallas kernels  53.2 us (97%)
  local copies, waits for them, and re-layouts  1.57 us (3%)
    pallas_call x1, Pallas kernels, body(): pl.pallas_call(functools.partial(kernel, scale), out_shape=jax.ShapeDtype...  53.2 us
    unnamed x1, local copies, waits for them, and re-layouts  1.57 us

profile of v7, /device:TPU:1, one launch (start us, length us, event | category | flops | bytes accessed | tf_op | source)
XLA Modules:
  0.0 54.8 jit_solution(5372405957276763679)
XLA Ops:
  0.0 53.2 %gram_band.1 = f32[256,128]{1,0:T(8,128)} custom-call(bf16[256,1024]{1,0:T(8,128)(2,1)} %sens.1, f32[2,128]{1,0:T(2,128)} %bitcast.7, f32[8,128]{1,0:T(8,128)} %bitcast.4, f32[8,128]{1,0:T(8,128)} %bitcast.5, f32[8,128]{1,0:T(8,128)} %bitcast.6), custom_call_target="tpu_custom_call" | custom-call | tf_op jit(solution)/shard_map/gram_band/pallas_call | solution.py:617
  53.2 1.6 %copy.7 = f32[256,128]{1,0:T(8,128)} copy(f32[256,128]{1,0:T(8,128)} %gram_band.1) | data formatting | bytes 262144

commit v8 on v7

--- a/solution.py
+++ b/solution.py
@@ -86,61 +86,6 @@
     def slab_rows(group):
         return pl.ds(group * GROUP, GROUP)
 
-    barrier = pltpu.get_barrier_semaphore()
-
-    def greet(cells, dp):
-        pl.semaphore_signal(barrier, inc=1, device_id=(cells, dp), device_id_type=MESH)
-
-    def when(*conditions):
-        return pl.when(functools.reduce(jnp.logical_and, conditions))
-
-    for j in range(1, 8):
-        greet(peer(j), d)
-    greet(c, d + 1 - 2 * odd)
-
-    @when(odd == 1, c >= 4, c < 6, top)
-    def _():
-        for j in range(1, 8):
-            greet(peer(j), block(-1))
-
-    @when(inner_top)
-    def _():
-        greet(c, block(2))
-
-        @pl.when(even)
-        def _():
-            greet(c, block(3))
-
-    @when(inner_top, odd == 1, c >= 4)
-    def _():
-        for j in range(1, 8):
-            greet(peer(j), block(2))
-
-    @when(bottom)
-    def _():
-        greet(c, block(COLUMN - 2))
-        greet(c, block(-2))
-
-        @pl.when(odd == 1)
-        def _():
-            greet(c, block(-3))
-            for j in range(1, 8):
-                greet(peer(j), block(-2))
-
-        @when(odd == 1, jnp.logical_not(last_column))
-        def _():
-            greet(c, block(COLUMN))
-
-
-    @when(top, even, jnp.logical_not(last_column))
-    def _():
-        greet(c, block(COLUMN))
-        greet(c, block(COLUMN + 1))
-
-    @when(top, first_column)
-    def _():
-        greet(c, block(-COLUMN - odd))
-
     own = [
         pltpu.make_async_copy(source, target, own_sem.at[i])
         for i, (source, target) in enumerate(
@@ -159,6 +104,62 @@
     for one in own:
         one.start()
 
+    barrier = pltpu.get_barrier_semaphore()
+
+    def greet(cells, dp):
+        pl.semaphore_signal(barrier, inc=1, device_id=(cells, dp), device_id_type=MESH)
+
+    def when(*conditions):
+        return pl.when(functools.reduce(jnp.logical_and, conditions))
+
+    for j in range(1, 8):
+        greet(peer(j), d)
+    greet(c, d + 1 - 2 * odd)
+
+    @when(odd == 1, c >= 4, c < 6, top)
+    def _():
+        for j in range(1, 8):
+            greet(peer(j), block(-1))
+
+    @when(inner_top)
+    def _():
+        greet(c, block(2))
+
+        @pl.when(even)
+        def _():
+            greet(c, block(3))
+
+    @when(inner_top, odd == 1, c >= 4)
+    def _():
+        for j in range(1, 8):
+            greet(peer(j), block(2))
+
+    @when(bottom)
+    def _():
+        greet(c, block(COLUMN - 2))
+        greet(c, block(-2))
+
+        @pl.when(odd == 1)
+        def _():
+            greet(c, block(-3))
+            for j in range(1, 8):
+                greet(peer(j), block(-2))
+
+        @when(odd == 1, jnp.logical_not(last_column))
+        def _():
+            greet(c, block(COLUMN))
+
+
+    @when(top, even, jnp.logical_not(last_column))
+    def _():
+        greet(c, block(COLUMN))
+        greet(c, block(COLUMN + 1))
+
+    @when(top, first_column)
+    def _():
+        greet(c, block(-COLUMN - odd))
+
+
     def count(*conditions):
         return functools.reduce(jnp.logical_and, conditions).astype(jnp.int32)
 
@@ -534,7 +535,7 @@
         value = far[0]
         for s in range(1, 8):
             value = value + far[s]
-        out[...] = value * scale
+        landing[...] = value * scale
 
     @pl.when(jnp.logical_not(from_far))
     def _():
@@ -549,7 +550,9 @@
         def _():
             landed(c).wait_recv()
 
-        out[...] = landing[...]
+
+    final = pltpu.make_async_copy(landing, out, own_sem.at[0])
+    final.start()
 
     for j in range(1, 8):
         coef_copy(j).wait_send()
@@ -607,18 +610,19 @@
         def _():
             on_each_half(4, 3, None, lambda one: one.wait_send(), lambda half: None)
 
+    final.wait()
+
 
 def body(sensitivity, weights, coef_x, coef_y, coef_z):
     rows, cells = sensitivity.shape
     part = rows // 8
     scale = float(cells * lax.axis_size("cells")) ** (-0.5)
-    vmem = pl.BlockSpec(memory_space=pltpu.VMEM)
     dma = pltpu.SemaphoreType.DMA
     return pl.pallas_call(
         functools.partial(kernel, scale),
         out_shape=jax.ShapeDtypeStruct((rows, rows // 2), jnp.float32),
         in_specs=[pl.BlockSpec(memory_space=pl.ANY)] * 5,
-        out_specs=vmem,
+        out_specs=pl.BlockSpec(memory_space=pl.ANY),
         scratch_shapes=[
             pltpu.VMEM((2, CZ), jnp.float32),
             pltpu.VMEM((8, 24, CZ), jnp.float32),

time: 55 us -> 54.4 us (0.989)
  Pallas kernels: 53.2 us -> 52.2 us
    pallas_call x1, Pallas kernels: 53.2 us -> 52.2 us  [body(): pl.pallas_call(functools.partial(kernel, scale), out_shape=jax.ShapeDtype...]
where the time goes in v8:
time: 54.4 us; the launch traced here: 53.8 us
  Pallas kernels  52.2 us (96%)
  local copies, waits for them, and re-layouts  1.57 us (3%)
    pallas_call x1, Pallas kernels, body(): pl.pallas_call(functools.partial(kernel, scale), out_shape=jax.ShapeDtype...  52.2 us
    unnamed x1, local copies, waits for them, and re-layouts  1.57 us

profile of v8, /device:TPU:1, one launch (start us, length us, event | category | flops | bytes accessed | tf_op | source)
XLA Modules:
  0.0 53.8 jit_solution(10705610971512082049)
XLA Ops:
  0.0 52.2 %gram_band.1 = f32[256,128]{1,0:T(8,128)} custom-call(bf16[256,1024]{1,0:T(8,128)(2,1)} %sens.1, f32[2,128]{1,0:T(2,128)} %bitcast.7, f32[8,128]{1,0:T(8,128)} %bitcast.4, f32[8,128]{1,0:T(8,128)} %bitcast.5, f32[8,128]{1,0:T(8,128)} %bitcast.6), custom_call_target="tpu_custom_call" | custom-call | tf_op jit(solution)/shard_map/gram_band/pallas_call | solution.py:621
  52.2 1.6 %copy.7 = f32[256,128]{1,0:T(8,128)} copy(f32[256,128]{1,0:T(8,128)} %gram_band.1) | data formatting | bytes 262144

commit v9 on v8

--- a/solution.py
+++ b/solution.py
@@ -518,8 +518,8 @@
             tile(PANEL, 1, 1)
             tile(0, 1, 3)
             reduce(0, 0)
+            reduce(1, 1)
             reduce(2, 2, block(-2))
-            reduce(1, 1)
             reduce(3, 3, block(-2))
 
         @pl.when(top)

time: 54.4 us -> 54.4 us (level)
  no operation moved by 1% of the time
where the time goes in v9:
time: 54.4 us; the launch traced here: 53.8 us
  Pallas kernels  52.2 us (96%)
  local copies, waits for them, and re-layouts  1.57 us (3%)
    pallas_call x1, Pallas kernels, body(): pl.pallas_call(functools.partial(kernel, scale), out_shape=jax.ShapeDtype...  52.2 us
    unnamed x1, local copies, waits for them, and re-layouts  1.57 us

profile of v9, /device:TPU:1, one launch (start us, length us, event | category | flops | bytes accessed | tf_op | source)
XLA Modules:
  0.0 53.8 jit_solution(10056982113806745133)
XLA Ops:
  0.0 52.2 %gram_band.1 = f32[256,128]{1,0:T(8,128)} custom-call(bf16[256,1024]{1,0:T(8,128)(2,1)} %sens.1, f32[2,128]{1,0:T(2,128)} %bitcast.7, f32[8,128]{1,0:T(8,128)} %bitcast.4, f32[8,128]{1,0:T(8,128)} %bitcast.5, f32[8,128]{1,0:T(8,128)} %bitcast.6), custom_call_target="tpu_custom_call" | custom-call | tf_op jit(solution)/shard_map/gram_band/pallas_call | solution.py:621
  52.2 1.6 %copy.7 = f32[256,128]{1,0:T(8,128)} copy(f32[256,128]{1,0:T(8,128)} %gram_band.1) | data formatting | bytes 262144
